TPU v7x, 512 devices: a whole 4x8x8 slice. The times are simulated.
512 devices in a mesh: dp: 64 (over z, y_lo, core), tensor: 8 (over x, y_hi).
Axes of the slice: x: 4, y: 8 (y_hi: 2, y_lo: 4; y = y_hi * 4 + y_lo), z: 8, core: 2. Of those that a mesh axis runs over, the one named last changes fastest.
Arguments:
- token_features: bfloat16 [12288, 5120], P(('dp', 'tensor')), may hold values from -6 to 6
- key_cotangent: bfloat16 [12288, 1024], P('dp', 'tensor'), may hold values from -6 to 6
- weight_master: float32 [5120, 1024], P('dp', 'tensor'), may hold values from -20 to 20
- weight_first: float32 [5120, 1024], P('dp', 'tensor'), may hold values from -24 to 24
- weight_second: float32 [5120, 1024], P('dp', 'tensor'), may hold values from 1 to 100
- gain_master_copy: float32 [128, 8], P('dp', 'tensor'), may hold values from 0.25 to 1.75
- gain_first_moment: float32 [128, 8], P('dp', 'tensor'), may hold values from -24 to 24
- gain_second_moment: float32 [128, 8], P('dp', 'tensor'), may hold values from 1 to 100
- weight_grad_prev: bfloat16 [64, 5120, 1024], P('dp', None, 'tensor'), may hold values from -16 to 16
- prior_gain_gradient: float32 [64, 128, 8], P('dp', None, 'tensor'), may hold values from -16 to 16
Outputs:
- input_grad: bfloat16 [12288, 5120], P(('dp', 'tensor'))
- weight_grad: bfloat16 [64, 5120, 1024], P('dp', None, 'tensor')
- gain_grad: float32 [64, 128, 8], P('dp', None, 'tensor')
- new_weight: float32 [5120, 1024], P('dp', 'tensor')
- new_weight_first: float32 [5120, 1024], P('dp', 'tensor')
- new_weight_second: float32 [5120, 1024], P('dp', 'tensor')
- new_gain: float32 [128, 8], P('dp', 'tensor')
- new_gain_first: float32 [128, 8], P('dp', 'tensor')
- new_gain_second: float32 [128, 8], P('dp', 'tensor')
All inputs are finite; a program needn't handle non-finite values.
Results may differ from a plain program's by a relative error of at most 0.012.
Values may be sent and summed in bfloat16 or wider, within the bound.
No kernel may reach another device: no remote copies, remote signals or barrier semaphores. Data moves between devices by JAX's collectives and lax.ppermute only.
A program may use at most 64 MiB of HBM per device.

v0:
```python
import jax
import jax.numpy as jnp
from jax import lax
from jax.sharding import PartitionSpec as P

HEAD_WIDTH = 128
KEY_FEATURES = 1024


beta_one = 0.9
beta_two = 0.95
corr_one = 1.0 - 0.9**8
corr_two = 1.0 - 0.95**8
learn_rate = 0.02
weight_decay = 0.1
adam_eps = 1e-08
norm_eps = 1e-06


def adamw(param, first, second, grad, decay):
    first_new = beta_one * first + (1.0 - beta_one) * grad
    second_new = beta_two * second + (1.0 - beta_two) * grad * grad
    update = first_new / corr_one / (jnp.sqrt(second_new / corr_two) + adam_eps)
    return (param - learn_rate * (update + decay * param), first_new, second_new)


def local(
    token_features,
    key_cotangent,
    weight_master,
    weight_first,
    weight_second,
    gain_master_copy,
    gain_first_moment,
    gain_second_moment,
    weight_grad_prev,
    prior_gain_gradient,
):
    groups = lax.axis_size("tensor")
    weight_full, gain_full = (
        lax.all_gather(weight_master.astype(jnp.bfloat16), "dp", axis=0, tiled=True),
        lax.all_gather(gain_master_copy.astype(jnp.bfloat16), "dp", axis=0, tiled=True),
    )
    heads_here = gain_full.shape[1]
    gain_vec = gain_full.astype(jnp.float32).T.reshape(-1)
    whole = lax.all_gather(token_features, "tensor", axis=0, tiled=True)
    keys = jnp.dot(whole, weight_full, preferred_element_type=jnp.float32)
    cotangent = key_cotangent.astype(jnp.float32)
    scaled = cotangent * gain_vec
    squares, cross = lax.psum(
        (jnp.sum(keys * keys, axis=1), jnp.sum(scaled * keys, axis=1)), "tensor"
    )
    inv = 1.0 / jnp.sqrt(squares / KEY_FEATURES + norm_eps)
    normalized_keys = keys * inv[:, None]
    key_grad = (
        inv[:, None] * (scaled - normalized_keys * (inv * cross / KEY_FEATURES)[:, None])
    ).astype(jnp.bfloat16)
    weight_grad = lax.dot_general(
        whole, key_grad, (((0,), (0,)), ((), ())), preferred_element_type=jnp.float32
    ).astype(jnp.bfloat16)[None]
    gain_grad = jnp.sum(cotangent * normalized_keys, axis=0).reshape(heads_here, HEAD_WIDTH).T[None]
    partial_value = lax.dot_general(
        key_grad, weight_full, (((1,), (1,)), ((), ())), preferred_element_type=jnp.float32
    )
    own_rows = token_features.shape[0]
    blocks = partial_value.astype(jnp.bfloat16).reshape(groups, own_rows, partial_value.shape[1])
    received = lax.all_to_all(blocks, "tensor", split_axis=0, concat_axis=0, tiled=True)
    input_grad = jnp.sum(received.astype(jnp.float32), axis=0).astype(jnp.bfloat16)
    summed_pair = (
        lax.psum_scatter(
            weight_grad_prev.astype(jnp.float32), "dp", scatter_dimension=1, tiled=True
        ),
        lax.psum_scatter(prior_gain_gradient, "dp", scatter_dimension=1, tiled=True),
    )
    summed_w = summed_pair[0][0]
    summed_g = summed_pair[1][0]
    new_weight, new_weight_first, new_weight_second = adamw(
        weight_master, weight_first, weight_second, summed_w, weight_decay
    )
    new_gain, new_gain_first, new_gain_second = adamw(
        gain_master_copy, gain_first_moment, gain_second_moment, summed_g, 0.0
    )
    return (
        input_grad,
        weight_grad,
        gain_grad,
        new_weight,
        new_weight_first,
        new_weight_second,
        new_gain,
        new_gain_first,
        new_gain_second,
    )


def solution(mesh):
    placed = (
        P(("dp", "tensor"), None),
        P("dp", "tensor"),
        P("dp", "tensor"),
        P("dp", "tensor"),
        P("dp", "tensor"),
        P("dp", "tensor"),
        P("dp", "tensor"),
        P("dp", "tensor"),
        P("dp", None, "tensor"),
        P("dp", None, "tensor"),
    )
    return jax.shard_map(
        local,
        mesh=mesh,
        in_specs=placed,
        out_specs=(
            P(("dp", "tensor"), None),
            P("dp", None, "tensor"),
            P("dp", None, "tensor"),
            P("dp", "tensor"),
            P("dp", "tensor"),
            P("dp", "tensor"),
            P("dp", "tensor"),
            P("dp", "tensor"),
            P("dp", "tensor"),
        ),
        check_vma=False,
    )
```

profile of v0, /device:TPU:1, one launch (start us, length us, event | category | flops | bytes accessed | tf_op | source)
XLA Modules:
  0.0 703.5 jit_solution(6296716240107310375)
XLA Ops:
  8.0 0.0 reduce-scatter.3.cloned.1.call-start
  8.1 3.0 convert_element_type.34
  11.0 0.0 copy-start.10
  11.0 0.0 copy-start.7
  11.0 0.0 copy-start.8
  11.1 0.0 copy-start.9
  11.1 0.0 reduce-scatter.3.cloned.1.call-update
  11.1 0.0 copy-start.2
  11.1 0.0 all-gather.3.cloned.1.call-start
  11.2 0.5 all-gather.3.cloned.1.call-update
  11.7 0.0 all-gather.5.cloned.1.call-start
  11.7 302.7 %reduce-scatter.3.cloned.1.call-done = f32[1,80,128]{2,1,0:T(8,128)} async-done(((f32[1,5120,128]{2,1,0:T(8,128)}), f32[1,80,128]{2,1,0:T(8,128)}) %reduce-scatter.3.cloned.1.call-update) | async-done | bytes 40976 | tf_op jit(solution)/shard_map/reduce_scatter | solution.py:70
  314.4 1.4 multiply_subtract_fusion
  315.9 0.0 all-gather.5.cloned.1.call-update
  315.9 0.6 fusion.13
  317.8 137.8 %all-reduce.1 = f32[1,128,1]{1,2,0:T(1,128)S(1)} all-reduce(f32[1,128,1]{1,2,0:T(1,128)S(1)} %copy-done.10), channel_id=3, replica_groups=mesh['dp'=64,'tensor'=8] {'dp'}, use_global_device_ids=true, to_apply=%region_7.0.clone | all-reduce | flops 128 | bytes 1024
  455.6 0.6 multiply_subtract_fusion.1
  456.3 0.2 dynamic-update-slice
  456.5 135.0 %all-reduce = bf16[128]{0:T(256)(128)(2,1)S(1)} all-reduce(bf16[128]{0:T(256)(128)(2,1)S(1)} %dynamic-update-slice), channel_id=1, replica_groups=mesh['dp'=64,'tensor'=8] {'dp'}, use_global_device_ids=true, to_apply=%add | all-reduce | flops 128 | bytes 512
  591.4 0.0 all-gather.3.cloned.1.call-done
  591.5 0.0 all-gather.5.cloned.1.call-done
  591.5 2.8 multiply_reduce_fusion
  594.3 29.8 %psum.14 = f32[192]{0:T(256)S(1)} all-reduce(f32[192]{0:T(256)S(1)} %get-tuple-element.39), channel_id=1, replica_groups=mesh['dp'=64,'tensor'=8] {'tensor'}, use_global_device_ids=true, to_apply=%region_1.0 | all-reduce | flops 192 | bytes 1536 | tf_op jit(solution)/shard_map/psum | solution.py:50
  624.1 0.6 fusion.6
  624.7 20.4 %psum.15 = f32[192]{0:T(256)S(1)} all-reduce(f32[192]{0:T(256)S(1)} %get-tuple-element.28), channel_id=1, replica_groups=mesh['dp'=64,'tensor'=8] {'tensor'}, use_global_device_ids=true, to_apply=%region_3.0 | all-reduce | flops 192 | bytes 1536 | tf_op jit(solution)/shard_map/psum | solution.py:50
  645.1 0.1 fusion.5
  645.2 2.0 convolution_convert_fusion
  647.2 7.0 %all-to-all-start = ((bf16[8,24,5120]{2,1,0:T(8,128)(2,1)}), bf16[8,24,5120]{2,1,0:T(8,128)(2,1)}, u32[]{:S(2)}, u32[]{:S(2)}) async-start(bf16[8,24,5120]{2,1,0:T(8,128)(2,1)} %bitcast.35), calls=%async_computation | async-start | bytes 3932160 | tf_op jit(solution)/shard_map/all_to_all | solution.py:67
  654.2 0.5 fusion
  654.8 1.4 copy.20
  656.2 37.3 %all-to-all-done = bf16[8,24,5120]{2,1,0:T(8,128)(2,1)} async-done(((bf16[8,24,5120]{2,1,0:T(8,128)(2,1)}), bf16[8,24,5120]{2,1,0:T(8,128)(2,1)}, u32[]{:S(2)}, u32[]{:S(2)}) %all-to-all-start) | async-done | bytes 1966112 | tf_op jit(solution)/shard_map/all_to_all | solution.py:67
  693.5 2.6 reduce_sum.41
  (21 shorter events, 0.1 us)
Async XLA Ops:
  8.0 306.4 %reduce-scatter.3.cloned.1.call-start = ((), (), s32[]{:S(2)}) async-start(), calls=%async_computation.4 | async-start | bytes 2662400 | tf_op jit(solution)/shard_map/reduce_scatter | solution.py:70
  11.0 303.4 %copy-start.3 = (f32[80,128]{1,0:T(8,128)S(1)}, f32[80,128]{1,0:T(8,128)}, u32[]{:S(2)}) copy-start(f32[80,128]{1,0:T(8,128)} %param.12) | copy-start | bytes 122884
  11.0 303.4 %copy-start.4 = (f32[80,128]{1,0:T(8,128)S(1)}, f32[80,128]{1,0:T(8,128)}, u32[]{:S(2)}) copy-start(f32[80,128]{1,0:T(8,128)} %param.13) | copy-start | bytes 122884
  11.0 303.4 %copy-start.5 = (f32[80,128]{1,0:T(8,128)S(1)}, f32[80,128]{1,0:T(8,128)}, u32[]{:S(2)}) copy-start(f32[80,128]{1,0:T(8,128)} %param.14) | copy-start | bytes 122884
  11.0 304.9 %copy-start.6 = (u32[512]{0:T(512)S(1)}, u32[512]{0:T(512)}, u32[]{:S(2)}) copy-start(u32[512]{0:T(512)} %constant.51) | copy-start | bytes 6148
  11.0 306.8 %copy-start.10 = (f32[1,128,1]{1,2,0:T(1,128)S(1)}, f32[1,128,1]{1,2,0:T(1,128)}, u32[]{:S(2)}) copy-start(f32[1,128,1]{1,2,0:T(1,128)} %param.19) | copy-start | bytes 1540
  11.0 444.6 %copy-start.7 = (f32[2,1]{0,1:T(1,128)S(1)}, f32[2,1]{0,1:T(1,128)}, u32[]{:S(2)}) copy-start(f32[2,1]{0,1:T(1,128)} %param.15) | copy-start | bytes 28
  11.0 444.6 %copy-start.8 = (f32[2,1]{0,1:T(1,128)S(1)}, f32[2,1]{0,1:T(1,128)}, u32[]{:S(2)}) copy-start(f32[2,1]{0,1:T(1,128)} %param.16) | copy-start | bytes 28
  11.1 444.6 %copy-start.9 = (f32[2,1]{0,1:T(1,128)S(1)}, f32[2,1]{0,1:T(1,128)}, u32[]{:S(2)}) copy-start(f32[2,1]{0,1:T(1,128)} %param.17) | copy-start | bytes 28
  11.1 613.0 %copy-start.2 = (bf16[192,128]{1,0:T(8,128)(2,1)S(1)}, bf16[192,128]{1,0:T(8,128)(2,1)}, u32[]{:S(2)}) copy-start(bf16[192,128]{1,0:T(8,128)(2,1)} %param.11) | copy-start | bytes 147460
  11.1 580.3 %all-gather.3.cloned.1.call-start = ((), (), s32[]{:S(2)}) async-start(), calls=%async_computation.2 | async-start | bytes 2211840 | tf_op jit(solution)/shard_map/all_gather | solution.py:46
  11.7 579.8 %all-gather.5.cloned.1.call-start = ((), (), s32[]{:S(2)}) async-start(), calls=%async_computation.3 | async-start | bytes 1331200 | tf_op jit(solution)/shard_map/all_gather | solution.py:41
  591.5 53.7 %copy-start.1 = (bf16[5120,128]{1,0:T(8,128)(2,1)S(1)}, bf16[5120,128]{1,0:T(8,128)(2,1)}, u32[]{:S(2)}) copy-start(bf16[5120,128]{1,0:T(8,128)(2,1)} %all-gather.5.cloned.1.call-done) | copy-start | bytes 3932164
  647.2 7.0 %copy-start = (bf16[192,5120]{1,0:T(8,128)(2,1)S(1)}, bf16[192,5120]{1,0:T(8,128)(2,1)}, u32[]{:S(2)}) copy-start(bf16[192,5120]{1,0:T(8,128)(2,1)} %all-gather.3.cloned.1.call-done) | copy-start | bytes 5898244
  647.2 46.3 %all-to-all-start = ((bf16[8,24,5120]{2,1,0:T(8,128)(2,1)}), bf16[8,24,5120]{2,1,0:T(8,128)(2,1)}, u32[]{:S(2)}, u32[]{:S(2)}) async-start(bf16[8,24,5120]{2,1,0:T(8,128)(2,1)} %bitcast.35), calls=%async_computation | async-start | bytes 3932160 | tf_op jit(solution)/shard_map/all_to_all | solution.py:67
Sparse Core Ops, SparseCore 0:
  11.6 302.7 reduce-scatter.2
Sparse Core Ops, SparseCore 1:
  14.8 79.4 all-gather.2
  316.0 121.8 all-gather.4
where the time goes:
time: 704 us
  waiting for transfers between devices  341 us (48%)
  blocking collectives  323 us (46%)
  between operations  16.9 us (2%)
  other arithmetic  8.37 us (1%)
  starting transfers between devices  7.16 us (1%)
    reduce_scatter x1, waiting for transfers between devices, local(): lax.psum_scatter(weight_grad_prev.astype(jnp.float32), 'dp', scatter_dime...  303 us
    unnamed x2, blocking collectives  273 us
    psum x2, blocking collectives, local(): lax.psum((jnp.sum(keys * keys, axis=1), jnp.sum(scaled * keys, axis=1)),...  50.2 us
    all_to_all x1, waiting for transfers between devices, local(): lax.all_to_all(blocks, 'tensor', split_axis=0, concat_axis=0, tiled=True)  37.3 us
  transfers between devices with their start and end apart: 4, of which 2 were waited for; matrix products, arithmetic and copies ran while one was open for 1% of the time, Pallas kernels for 0%

commit v1 on v0

v1 whole, which is shorter than its diff:
```python
import jax
import jax.numpy as jnp
from jax import lax
from jax.sharding import Mesh, PartitionSpec as P

HEAD_WIDTH = 128
KEY_FEATURES = 1024

beta_one = 0.9
beta_two = 0.95
corr_one = 1.0 - 0.9**8
corr_two = 1.0 - 0.95**8
learn_rate = 0.02
weight_decay = 0.1
adam_eps = 1e-08
norm_eps = 1e-06

NZ, NYL, NC, NX, NYH = 8, 4, 2, 4, 2
ROWS = 80
EXT = 88
SWAP = [(0, 1), (1, 0)]
f32, bf16 = jnp.float32, jnp.bfloat16


def adamw(param, first, second, grad, decay):
    first_new = beta_one * first + (1.0 - beta_one) * grad
    second_new = beta_two * second + (1.0 - beta_two) * grad * grad
    update = first_new / corr_one / (jnp.sqrt(second_new / corr_two) + adam_eps)
    return (param - learn_rate * (update + decay * param), first_new, second_new)


def pick(array, index, axis):
    return lax.dynamic_index_in_dim(array, index, axis, keepdims=False)


def ordered(mine, other, index):
    return jnp.where(index == 0, jnp.stack([mine, other]), jnp.stack([other, mine]))


def local(
    token_features,
    key_cotangent,
    weight_master,
    weight_first,
    weight_second,
    gain_master_copy,
    gain_first_moment,
    gain_second_moment,
    weight_grad_prev,
    prior_gain_gradient,
):
    c = lax.axis_index("c")
    yh = lax.axis_index("yh")
    own, width = token_features.shape
    half = NX * own

    prev = weight_grad_prev.reshape(NZ * NYL, NC, ROWS, 128)
    gain_prev = prior_gain_gradient.reshape(NZ * NYL, NC, 2)
    hi = gain_prev.astype(bf16)
    mid = (gain_prev - hi.astype(f32)).astype(bf16)
    low = (gain_prev - hi.astype(f32) - mid.astype(f32)).astype(bf16)
    split = jnp.concatenate([hi, mid, low], axis=-1)[:, :, None, :]
    split = jnp.pad(split, ((0, 0), (0, 0), (0, EXT - ROWS - 1), (0, 128 - 6)))
    keep = jnp.concatenate([pick(prev, c, 1), pick(split, c, 1)], axis=1)
    give = jnp.concatenate([pick(prev, 1 - c, 1), pick(split, 1 - c, 1)], axis=1)
    got = lax.ppermute(give, "c", SWAP)
    pair = keep.astype(f32) + got.astype(f32)
    sum_z = lax.psum_scatter(pair, "z", scatter_dimension=0, tiled=True)
    sum_all = lax.psum_scatter(sum_z, "yl", scatter_dimension=0, tiled=True)[0]

    gain_row = jnp.pad(gain_master_copy.astype(bf16).reshape(1, 2), ((0, EXT - ROWS - 1), (0, 126)))
    shard = jnp.concatenate([weight_master.astype(bf16), gain_row], axis=0)
    group = ("z", "yh", "yl")
    many = NZ * NYH * NYL
    gathered = lax.all_to_all(
        jnp.broadcast_to(shard[None], (many, EXT, 128)), group, 0, 0, tiled=True
    )
    gathered_other = lax.ppermute(gathered, "c", SWAP)
    both = ordered(gathered, gathered_other, c).reshape(NC, NZ, NYH, NYL, EXT, 128)
    both = both.transpose(2, 1, 3, 0, 4, 5)
    weight_two = both[:, :, :, :, :ROWS].reshape(NYH, width, 128)
    gain_two = both[:, :, :, :, ROWS, :2].reshape(NYH, 128).astype(f32)

    cot = key_cotangent.reshape(NX, NYH, own, 128)
    cot_got = lax.ppermute(pick(cot, 1 - yh, 1), "yh", SWAP)
    cot_two = ordered(pick(cot, yh, 1), cot_got, yh).reshape(NYH, half, 128).astype(f32)

    rows = lax.all_gather(token_features, "x", axis=0, tiled=True)
    partner = lax.ppermute(token_features, "yh", SWAP)
    rows_partner = lax.all_gather(partner, "x", axis=0, tiled=True)

    keys = [jnp.dot(rows, weight_two[h], preferred_element_type=f32) for h in range(NYH)]
    scaled = [cot_two[h] * gain_two[h] for h in range(NYH)]
    sums = jnp.stack(
        [
            sum(jnp.sum(k * k, axis=1) for k in keys),
            sum(jnp.sum(s * k, axis=1) for s, k in zip(scaled, keys)),
        ]
    )
    sums = lax.all_to_all(jnp.broadcast_to(sums[None], (NX, 2, half)), "x", 0, 0, tiled=True)
    squares, cross = jnp.sum(sums, axis=0)
    inv = 1.0 / jnp.sqrt(squares / KEY_FEATURES + norm_eps)
    normed = [k * inv[:, None] for k in keys]
    factor = (inv * cross / KEY_FEATURES)[:, None]
    grads = [(inv[:, None] * (s - n * factor)).astype(bf16) for s, n in zip(scaled, normed)]
    gain_terms = jnp.stack([jnp.sum(cot_two[h] * normed[h], axis=0) for h in range(NYH)])

    terms = sum(
        lax.dot_general(grads[h], weight_two[h], (((1,), (1,)), ((), ())), preferred_element_type=f32)
        for h in range(NYH)
    )
    received = lax.all_to_all(terms.astype(bf16).reshape(NX, own, width), "x", 0, 0, tiled=True)
    input_grad = jnp.sum(received.astype(f32), axis=0).astype(bf16)

    both_grads = jnp.stack(grads)
    grad_partner = lax.ppermute(pick(both_grads, 1 - yh, 0), "yh", SWAP)
    gain_partner = lax.ppermute(pick(gain_terms, 1 - yh, 0), "yh", SWAP)
    contract = (((0,), (0,)), ((), ()))
    weight_grad = (
        lax.dot_general(rows, pick(both_grads, yh, 0), contract, preferred_element_type=f32)
        + lax.dot_general(rows_partner, grad_partner, contract, preferred_element_type=f32)
    ).astype(bf16)[None]
    gain_grad = (pick(gain_terms, yh, 0) + gain_partner).reshape(1, 128, 1)

    summed_w = sum_all[:ROWS]
    summed_g = (sum_all[ROWS, 0:2] + sum_all[ROWS, 2:4] + sum_all[ROWS, 4:6]).reshape(2, 1)
    new_weight = adamw(weight_master, weight_first, weight_second, summed_w, weight_decay)
    new_gain = adamw(gain_master_copy, gain_first_moment, gain_second_moment, summed_g, 0.0)
    return (input_grad, weight_grad, gain_grad, *new_weight, *new_gain)


def solution(mesh):
    fine = Mesh(mesh.devices.reshape(NZ, NYL, NC, NX, NYH), ("z", "yl", "c", "x", "yh"))
    dp, tensor = ("z", "yl", "c"), ("x", "yh")
    state = P(dp, tensor)
    stacked = P(dp, None, tensor)
    tokens = P(dp + tensor, None)
    return jax.shard_map(
        local,
        mesh=fine,
        in_specs=(tokens,) + (state,) * 7 + (stacked, stacked),
        out_specs=(tokens, stacked, stacked) + (state,) * 6,
        check_vma=False,
    )
```

time: 704 us -> 259 us (0.37)
  the two profiles are of different devices: /device:TPU:1 before, /device:TPU:2 now
where the time goes in v1:
time: 259 us
  waiting for transfers between devices  109 us (42%)
  blocking collectives  75.7 us (29%)
  starting transfers between devices  33.6 us (13%)
  between operations  14.4 us (6%)
  local copies, waits for them, and re-layouts  12.8 us (5%)
  other arithmetic  9.23 us (4%)
  matrix products  4.1 us (2%)
    unnamed x3, waiting for transfers between devices  54.1 us
    reduce_scatter x1, waiting for transfers between devices, local(): sum_z = lax.psum_scatter(pair, 'z', scatter_dimension=0, tiled=True)  47.9 us
    all_to_all x1, blocking collectives, local(): lax.all_to_all(jnp.broadcast_to(shard[None], (many, EXT, 128)), group, 0,...  47.1 us
    all_gather x1, blocking collectives, local(): rows = lax.all_gather(token_features, 'x', axis=0, tiled=True)  14.7 us
    all_gather x1, blocking collectives, local(): rows_partner = lax.all_gather(partner, 'x', axis=0, tiled=True)  13.9 us
    all_to_all x1, starting transfers between devices, local(): lax.all_to_all(terms.astype(bf16).reshape(NX, own, width), 'x', 0, 0, til...  5.65 us
    ppermute x1, starting transfers between devices, local(): cot_got = lax.ppermute(pick(cot, 1 - yh, 1), 'yh', SWAP)  5.4 us
    ppermute x1, starting transfers between devices, local(): gain_partner = lax.ppermute(pick(gain_terms, 1 - yh, 0), 'yh', SWAP)  5.39 us
  transfers between devices with their start and end apart: 10, of which 4 were waited for; matrix products, arithmetic and copies ran while one was open for 6% of the time, Pallas kernels for 0%

profile of v1, /device:TPU:2, one launch (start us, length us, event | category | flops | bytes accessed | tf_op | source)
XLA Modules:
  0.0 258.6 jit_solution(2971514188689683008)
XLA Ops:
  7.8 1.3 reduce.4
  9.4 0.8 pad_dynamic-slice_fusion.1
  10.6 1.9 collective-permute-start.5
  12.6 2.0 collective-permute-done.5
  14.6 1.3 convert_add_fusion
  16.0 47.9 %reduce-scatter.2.cloned.1.call-done = f32[4,88,128]{2,1,0:T(8,128)} async-done(((f32[32,88,128]{2,1,0:T(8,128)}), f32[4,88,128]{2,1,0:T(8,128)}) %reduce-scatter.2.cloned.1.call-update) | async-done | bytes 180240 | tf_op jit(solution)/shard_map/reduce_scatter | solution.py:68
  64.0 1.3 dynamic-slice
  65.3 54.1 %all-reduce.5.cloned.1.call-done = f32[4,88,128]{2,1,0:T(8,128)} async-done(((f32[4,88,128]{2,1,0:T(8,128)}), f32[4,88,128]{2,1,0:T(8,128)}) %all-reduce.5.cloned.1.call-update) | async-done | bytes 180240
  119.3 1.4 dynamic-slice_bitcast_fusion.2
  120.8 0.6 multiply_subtract_fusion.1
  121.4 2.1 multiply_subtract_fusion
  123.7 47.1 %all_to_all.15 = bf16[64,88,128]{2,1,0:T(8,128)(2,1)S(1)} all-to-all(bf16[64,88,128]{2,1,0:T(8,128)(2,1)S(1)} %broadcast_in_dim.8), channel_id=1, replica_groups=mesh['z'=8,'yl'=4,'c'=2,'x'=4,'yh'=2] {'z','yh','yl'}, dimensions={0} | all-to-all | bytes 2883584 | tf_op jit(solution)/shard_map/all_to_all | solution.py:75
  170.8 1.9 collective-permute-start
  172.8 5.4 %collective-permute-start.1 = (bf16[4,24,128]{2,1,0:T(8,128)(2,1)S(1)}, bf16[4,24,128]{2,1,0:T(8,128)(2,1)S(1)}, u32[]{:S(2)}, u32[]{:S(2)}) collective-permute-start(bf16[4,24,128]{2,1,0:T(8,128)(2,1)S(1)} %get-tuple-element.93), channel_id=1, source_target_pairs={{0,1},{1,0},{2,3},{3,2},{4,5},{5,4},{6,7},{7,6},{8,9},{9,8},{10,11... | collective-permute-start | bytes 73736 | tf_op jit(solution)/shard_map/ppermute | solution.py:85
  178.2 4.4 %collective-permute-start.3 = (bf16[24,5120]{1,0:T(8,128)(2,1)S(1)}, bf16[24,5120]{1,0:T(8,128)(2,1)}, u32[]{:S(2)}, u32[]{:S(2)}) collective-permute-start(bf16[24,5120]{1,0:T(8,128)(2,1)S(1)} %copy-done.3), channel_id=1, source_target_pairs={{0,1},{1,0},{2,3},{3,2},{4,5},{5,4},{6,7},{7,6},{8,9},{9,8},{10,11... | collective-permute-start | bytes 737288 | tf_op jit(solution)/shard_map/ppermute | solution.py:89
  182.6 14.7 %all_gather.6 = bf16[96,5120]{1,0:T(8,128)(2,1)S(1)} all-gather(bf16[24,5120]{1,0:T(8,128)(2,1)S(1)} %copy-done.3), channel_id=1, replica_groups=mesh['z'=8,'yl'=4,'c'=2,'x'=4,'yh'=2] {'x'}, dimensions={0}, use_global_device_ids=true | all-gather | bytes 1228800 | tf_op jit(solution)/shard_map/all_gather | solution.py:88
  197.3 2.2 fusion.3
  199.5 1.2 fusion.28
  200.8 1.2 copy.86
  202.3 1.4 copy.85
  204.2 0.9 copy-done
  205.6 0.6 broadcast_in_dim.9
  206.2 4.5 %all-to-all-start.1 = ((f32[4,2,96]{2,1,0:T(2,128)}), f32[4,2,96]{2,1,0:T(2,128)S(1)}, u32[]{:S(2)}, u32[]{:S(2)}) async-start(f32[4,2,96]{2,1,0:T(2,128)} %broadcast_in_dim.9), calls=%async_computation.1 | async-start | bytes 8192 | tf_op jit(solution)/shard_map/all_to_all | solution.py:100
  210.7 13.9 %all_gather.7 = bf16[96,5120]{1,0:T(8,128)(2,1)S(1)} all-gather(bf16[24,5120]{1,0:T(8,128)(2,1)} %collective-permute-done.3), channel_id=1, replica_groups=mesh['z'=8,'yl'=4,'c'=2,'x'=4,'yh'=2] {'x'}, dimensions={0}, use_global_device_ids=true | all-gather | bytes 1228800 | tf_op jit(solution)/shard_map/all_gather | solution.py:90
  224.8 5.4 %collective-permute-start.4 = (f32[128]{0:T(128)S(1)}, f32[128]{0:T(128)S(1)}, u32[]{:S(2)}, u32[]{:S(2)}) collective-permute-start(f32[128]{0:T(128)S(1)} %fusion.22), channel_id=1, source_target_pairs={{0,1},{1,0},{2,3},{3,2},{4,5},{5,4},{6,7},{7,6},{8,9},{9,8},{10,11... | collective-permute-start | bytes 1544 | tf_op jit(solution)/shard_map/ppermute | solution.py:117
  230.8 0.8 copy-done.1
  231.5 1.5 fusion.1
  233.0 5.6 %all-to-all-start.2 = ((bf16[4,24,5120]{2,1,0:T(8,128)(2,1)}), bf16[4,24,5120]{2,1,0:T(8,128)(2,1)S(1)}, u32[]{:S(2)}, u32[]{:S(2)}) async-start(bf16[4,24,5120]{2,1,0:T(8,128)(2,1)} %bitcast.124), calls=%async_computation.2 | async-start | bytes 1966080 | tf_op jit(solution)/shard_map/all_to_all | solution.py:112
  239.3 4.4 %collective-permute-start.2 = (bf16[96,128]{1,0:T(8,128)(2,1)S(1)}, bf16[96,128]{1,0:T(8,128)(2,1)S(1)}, u32[]{:S(2)}, u32[]{:S(2)}) collective-permute-start(bf16[96,128]{1,0:T(8,128)(2,1)S(1)} %fusion.10), channel_id=1, source_target_pairs={{0,1},{1,0},{2,3},{3,2},{4,5},{5,4},{6,7},{7,6},{8,9},{9,8},{10,11... | collective-permute-start | bytes 73736 | tf_op jit(solution)/shard_map/ppermute | solution.py:116
  244.2 4.7 %collective-permute-done.2 = bf16[96,128]{1,0:T(8,128)(2,1)S(1)} collective-permute-done((bf16[96,128]{1,0:T(8,128)(2,1)S(1)}, bf16[96,128]{1,0:T(8,128)(2,1)S(1)}, u32[]{:S(2)}, u32[]{:S(2)}) %collective-permute-start.2) | collective-permute-done | bytes 24608 | tf_op jit(solution)/shard_map/ppermute | solution.py:116
  249.4 1.4 copy.100
  250.9 0.9 reduce_sum.80
  (67 shorter events, 5.4 us)
Async XLA Ops:
  7.2 3.2 %copy-start.2 = (bf16[1,5120,128]{2,1,0:T(8,128)(2,1)S(1)}, bf16[1,5120,128]{2,1,0:T(8,128)(2,1)}, u32[]{:S(2)}) copy-start(bf16[1,5120,128]{2,1,0:T(8,128)(2,1)} %param.18) | copy-start | bytes 3932164
  7.2 56.8 %reduce-scatter.2.cloned.1.call-start = ((), (), s32[]{:S(2)}) async-start(), calls=%async_computation.4 | async-start | bytes 1622016 | tf_op jit(solution)/shard_map/reduce_scatter | solution.py:68
  10.6 4.1 %collective-permute-start.5 = (bf16[32,88,128]{2,1,0:T(8,128)(2,1)S(1)}, bf16[32,88,128]{2,1,0:T(8,128)(2,1)S(1)}, u32[]{:S(2)}, u32[]{:S(2)}) collective-permute-start(bf16[32,88,128]{2,1,0:T(8,128)(2,1)S(1)} %pad_maximum_fusion), channel_id=1, source_target_pairs={{0,8},{8,0},{1,9},{9,1},{2,10},{10,2},{3,11},{11,3},{4,12},{12,4},... | collective-permute-start | bytes 2162696 | tf_op jit(solution)/shard_map/ppermute | solution.py:66
  15.9 104.9 %copy-start.8 = (f32[2,1]{0,1:T(1,128)S(1)}, f32[2,1]{0,1:T(1,128)}, u32[]{:S(2)}) copy-start(f32[2,1]{0,1:T(1,128)} %param.15) | copy-start | bytes 28
  15.9 104.9 %copy-start.9 = (f32[2,1]{0,1:T(1,128)S(1)}, f32[2,1]{0,1:T(1,128)}, u32[]{:S(2)}) copy-start(f32[2,1]{0,1:T(1,128)} %param.16) | copy-start | bytes 28
  15.9 104.9 %copy-start.10 = (f32[2,1]{0,1:T(1,128)S(1)}, f32[2,1]{0,1:T(1,128)}, u32[]{:S(2)}) copy-start(f32[2,1]{0,1:T(1,128)} %param.17) | copy-start | bytes 28
  15.9 105.5 %copy-start.5 = (f32[80,128]{1,0:T(8,128)S(1)}, f32[80,128]{1,0:T(8,128)}, u32[]{:S(2)}) copy-start(f32[80,128]{1,0:T(8,128)} %param.12) | copy-start | bytes 122884
  15.9 105.5 %copy-start.6 = (f32[80,128]{1,0:T(8,128)S(1)}, f32[80,128]{1,0:T(8,128)}, u32[]{:S(2)}) copy-start(f32[80,128]{1,0:T(8,128)} %param.13) | copy-start | bytes 122884
  15.9 105.5 %copy-start.7 = (f32[80,128]{1,0:T(8,128)S(1)}, f32[80,128]{1,0:T(8,128)}, u32[]{:S(2)}) copy-start(f32[80,128]{1,0:T(8,128)} %param.14) | copy-start | bytes 122884
  16.0 103.4 %all-reduce.5.cloned.1.call-start = ((), (), s32[]{:S(2)}) async-start(), calls=%async_computation.5 | async-start | bytes 360448
  123.7 49.0 %copy-start.4 = (bf16[192,128]{1,0:T(8,128)(2,1)S(1)}, bf16[192,128]{1,0:T(8,128)(2,1)}, u32[]{:S(2)}) copy-start(bf16[192,128]{1,0:T(8,128)(2,1)} %param.11) | copy-start | bytes 147460
  123.7 54.5 %copy-start.3 = (bf16[24,5120]{1,0:T(8,128)(2,1)S(1)}, bf16[24,5120]{1,0:T(8,128)(2,1)}, u32[]{:S(2)}) copy-start(bf16[24,5120]{1,0:T(8,128)(2,1)} %param.10) | copy-start | bytes 737284
  170.8 26.4 %collective-permute-start = (bf16[64,88,128]{2,1,0:T(8,128)(2,1)S(1)}, bf16[64,88,128]{2,1,0:T(8,128)(2,1)}, u32[]{:S(2)}, u32[]{:S(2)}) collective-permute-start(bf16[64,88,128]{2,1,0:T(8,128)(2,1)S(1)} %all_to_all.15), channel_id=1, source_target_pairs={{0,8},{8,0},{1,9},{9,1},{2,10},{10,2},{3,11},{11,3},{4,12},{12,4},... | collective-permute-start | bytes 4325384 | tf_op jit(solution)/shard_map/ppermute | solution.py:78
  172.8 24.5 %collective-permute-start.1 = (bf16[4,24,128]{2,1,0:T(8,128)(2,1)S(1)}, bf16[4,24,128]{2,1,0:T(8,128)(2,1)S(1)}, u32[]{:S(2)}, u32[]{:S(2)}) collective-permute-start(bf16[4,24,128]{2,1,0:T(8,128)(2,1)S(1)} %get-tuple-element.93), channel_id=1, source_target_pairs={{0,1},{1,0},{2,3},{3,2},{4,5},{5,4},{6,7},{7,6},{8,9},{9,8},{10,11... | collective-permute-start | bytes 73736 | tf_op jit(solution)/shard_map/ppermute | solution.py:85
  178.2 32.5 %collective-permute-start.3 = (bf16[24,5120]{1,0:T(8,128)(2,1)S(1)}, bf16[24,5120]{1,0:T(8,128)(2,1)}, u32[]{:S(2)}, u32[]{:S(2)}) collective-permute-start(bf16[24,5120]{1,0:T(8,128)(2,1)S(1)} %copy-done.3), channel_id=1, source_target_pairs={{0,1},{1,0},{2,3},{3,2},{4,5},{5,4},{6,7},{7,6},{8,9},{9,8},{10,11... | collective-permute-start | bytes 737288 | tf_op jit(solution)/shard_map/ppermute | solution.py:89
  203.7 1.3 copy-start
  206.2 18.4 %all-to-all-start.1 = ((f32[4,2,96]{2,1,0:T(2,128)}), f32[4,2,96]{2,1,0:T(2,128)S(1)}, u32[]{:S(2)}, u32[]{:S(2)}) async-start(f32[4,2,96]{2,1,0:T(2,128)} %broadcast_in_dim.9), calls=%async_computation.1 | async-start | bytes 8192 | tf_op jit(solution)/shard_map/all_to_all | solution.py:100
  224.8 18.8 %collective-permute-start.4 = (f32[128]{0:T(128)S(1)}, f32[128]{0:T(128)S(1)}, u32[]{:S(2)}, u32[]{:S(2)}) collective-permute-start(f32[128]{0:T(128)S(1)} %fusion.22), channel_id=1, source_target_pairs={{0,1},{1,0},{2,3},{3,2},{4,5},{5,4},{6,7},{7,6},{8,9},{9,8},{10,11... | collective-permute-start | bytes 1544 | tf_op jit(solution)/shard_map/ppermute | solution.py:117
  230.2 1.3 copy-start.1
  233.0 17.8 %all-to-all-start.2 = ((bf16[4,24,5120]{2,1,0:T(8,128)(2,1)}), bf16[4,24,5120]{2,1,0:T(8,128)(2,1)S(1)}, u32[]{:S(2)}, u32[]{:S(2)}) async-start(bf16[4,24,5120]{2,1,0:T(8,128)(2,1)} %bitcast.124), calls=%async_computation.2 | async-start | bytes 1966080 | tf_op jit(solution)/shard_map/all_to_all | solution.py:112
  239.3 9.6 %collective-permute-start.2 = (bf16[96,128]{1,0:T(8,128)(2,1)S(1)}, bf16[96,128]{1,0:T(8,128)(2,1)S(1)}, u32[]{:S(2)}, u32[]{:S(2)}) collective-permute-start(bf16[96,128]{1,0:T(8,128)(2,1)S(1)} %fusion.10), channel_id=1, source_target_pairs={{0,1},{1,0},{2,3},{3,2},{4,5},{5,4},{6,7},{7,6},{8,9},{9,8},{10,11... | collective-permute-start | bytes 73736 | tf_op jit(solution)/shard_map/ppermute | solution.py:116
Sparse Core Ops, SparseCore 0:
  16.1 47.8 reduce-scatter.1
  66.9 52.4 all-reduce.4

commit v2 on v1

v2 whole, which is shorter than its diff:
```python
import jax
import jax.numpy as jnp
from jax import lax
from jax.sharding import Mesh, PartitionSpec as P

HEAD_WIDTH = 128
KEY_FEATURES = 1024

beta_one = 0.9
beta_two = 0.95
corr_one = 1.0 - 0.9**8
corr_two = 1.0 - 0.95**8
learn_rate = 0.02
weight_decay = 0.1
adam_eps = 1e-08
norm_eps = 1e-06

NZ, NYL, NC, NX, NYH = 8, 4, 2, 4, 2
ROWS = 80
EXT = 88
SWAP = [(0, 1), (1, 0)]
f32, bf16 = jnp.float32, jnp.bfloat16


def adamw(param, first, second, grad, decay):
    first_new = beta_one * first + (1.0 - beta_one) * grad
    second_new = beta_two * second + (1.0 - beta_two) * grad * grad
    update = first_new / corr_one / (jnp.sqrt(second_new / corr_two) + adam_eps)
    return (param - learn_rate * (update + decay * param), first_new, second_new)


def pick(array, index, axis):
    return lax.dynamic_index_in_dim(array, index, axis, keepdims=False)


def ordered(mine, other, index):
    return jnp.where(index == 0, jnp.stack([mine, other]), jnp.stack([other, mine]))


def split3(row, count):
    hi = row.astype(bf16)
    mid = (row - hi.astype(f32)).astype(bf16)
    low = (row - hi.astype(f32) - mid.astype(f32)).astype(bf16)
    index = lax.broadcasted_iota(jnp.int32, (count, 128), 0)
    zero = jnp.zeros((), bf16)
    rest = jnp.where(index == 2, mid, jnp.where(index == 3, low, zero))
    return jnp.where(index == 1, hi, rest)


def gather_x(block):
    return lax.all_gather(jnp.pad(block, ((0, 8), (0, 0))), "x", axis=0)


def used_rows(gathered, own):
    return gathered[:, :own].reshape(-1, gathered.shape[2])


def exchange_x(block_for, mine):
    return [mine] + [
        lax.ppermute(block_for(d), "x", [(i, (i + d) % NX) for i in range(NX)])
        for d in (2, 1, 3)
    ]


def local(
    token_features,
    key_cotangent,
    weight_master,
    weight_first,
    weight_second,
    gain_master_copy,
    gain_first_moment,
    gain_second_moment,
    weight_grad_prev,
    prior_gain_gradient,
):
    c = lax.axis_index("c")
    x = lax.axis_index("x")
    yh = lax.axis_index("yh")
    dp = lax.axis_index(("z", "yl", "c"))
    own, width = token_features.shape
    half = NX * own

    cot = key_cotangent.reshape(NX, NYH, own, 128)
    give_cot = pick(cot, 1 - yh, 1)
    packed = jnp.concatenate([token_features] + [give_cot[i] for i in range(NX)], axis=1)
    packed = lax.ppermute(packed, "yh", SWAP)
    partner = packed[:, :width]
    cot_got = packed[:, width:].reshape(own, NX, 128).transpose(1, 0, 2)

    place = lax.broadcasted_iota(jnp.int32, (EXT - ROWS, 128), 1)
    first = lax.broadcasted_iota(jnp.int32, (EXT - ROWS, 128), 0) == 0
    two = gain_master_copy.astype(bf16)
    zero = jnp.zeros((), bf16)
    gain_row = jnp.where(first & (place == 2 * dp), two[0, 0], zero)
    gain_row = jnp.where(first & (place == 2 * dp + 1), two[1, 0], gain_row)
    gain_row = gain_row + split3(prior_gain_gradient.reshape(1, 128), EXT - ROWS)
    shard = jnp.concatenate([weight_master.astype(bf16), gain_row], axis=0)
    shard, packed = lax.optimization_barrier((shard, packed))
    group = ("z", "yh", "yl")
    many = NZ * NYH * NYL
    gathered = lax.all_to_all(
        jnp.broadcast_to(shard[None], (many, EXT, 128)), group, 0, 0, tiled=True
    )

    rows = used_rows(gather_x(token_features), own)
    rows_partner = gather_x(partner)

    prev = weight_grad_prev.reshape(NZ * NYL * NC, ROWS, 128)
    prev, gathered = lax.optimization_barrier((prev, gathered))
    arrived = lax.all_to_all(prev, ("z", "yl", "c"), 0, 0, tiled=True)

    gathered_other = lax.ppermute(gathered, "c", SWAP)
    both = ordered(gathered, gathered_other, c).reshape(NC, NZ, NYH, NYL, EXT, 128)
    both = both.transpose(2, 1, 3, 0, 4, 5)
    weight_two = both[:, :, :, :, :ROWS].reshape(NYH, width, 128)
    extra = jnp.sum(both[:, :, :, :, ROWS:].astype(f32), axis=(1, 2, 3))
    gain_two = extra[:, 0]
    summed_g = jnp.sum(pick(extra, yh, 0)[1:4], axis=0)

    cot_two = ordered(pick(cot, yh, 1), cot_got, yh).reshape(NYH, half, 128).astype(f32)


    keys = [jnp.dot(rows, weight_two[h], preferred_element_type=f32) for h in range(NYH)]
    scaled = [cot_two[h] * gain_two[h] for h in range(NYH)]
    sums = jnp.stack(
        [
            sum(jnp.sum(k * k, axis=1) for k in keys),
            sum(jnp.sum(s * k, axis=1) for s, k in zip(scaled, keys)),
        ]
    )
    squares, cross = lax.psum(sums, "x")
    inv = 1.0 / jnp.sqrt(squares / KEY_FEATURES + norm_eps)
    normed = [k * inv[:, None] for k in keys]
    factor = (inv * cross / KEY_FEATURES)[:, None]
    grads = [(inv[:, None] * (s - n * factor)).astype(bf16) for s, n in zip(scaled, normed)]
    gain_terms = jnp.stack([jnp.sum(cot_two[h] * normed[h], axis=0) for h in range(NYH)])

    terms = sum(
        lax.dot_general(grads[h], weight_two[h], (((1,), (1,)), ((), ())), preferred_element_type=f32)
        for h in range(NYH)
    )
    terms = terms.astype(bf16).reshape(NX, own, width)
    received = exchange_x(lambda d: pick(terms, lax.rem(x + d, NX), 0), pick(terms, x, 0))
    input_grad = sum(block.astype(f32) for block in received).astype(bf16)

    both_grads = jnp.stack(grads)
    give = jnp.concatenate([both_grads[0], split3(gain_terms[0:1], 8)]), jnp.concatenate(
        [both_grads[1], split3(gain_terms[1:2], 8)]
    )
    got = lax.ppermute(jnp.where(yh == 0, give[1], give[0]), "yh", SWAP)
    rows_partner, got, input_grad = lax.optimization_barrier((rows_partner, got, input_grad))
    rows_partner = used_rows(rows_partner, own)
    contract = (((0,), (0,)), ((), ()))
    weight_grad = (
        lax.dot_general(rows, pick(both_grads, yh, 0), contract, preferred_element_type=f32)
        + lax.dot_general(rows_partner, got[:half], contract, preferred_element_type=f32)
    ).astype(bf16)[None]
    gain_partner = jnp.sum(got[half:].astype(f32), axis=0)
    gain_grad = (pick(gain_terms, yh, 0) + gain_partner).reshape(1, 128, 1)

    arrived, input_grad = lax.optimization_barrier((arrived, input_grad))
    summed_w = jnp.sum(arrived.astype(f32), axis=0)
    summed_g = lax.dynamic_slice(summed_g, (2 * dp,), (2,)).reshape(2, 1)
    new_weight = adamw(weight_master, weight_first, weight_second, summed_w, weight_decay)
    new_gain = adamw(gain_master_copy, gain_first_moment, gain_second_moment, summed_g, 0.0)
    return (input_grad, weight_grad, gain_grad, *new_weight, *new_gain)


def solution(mesh):
    fine = Mesh(mesh.devices.reshape(NZ, NYL, NC, NX, NYH), ("z", "yl", "c", "x", "yh"))
    dp, tensor = ("z", "yl", "c"), ("x", "yh")
    state = P(dp, tensor)
    stacked = P(dp, None, tensor)
    tokens = P(dp + tensor, None)
    return jax.shard_map(
        local,
        mesh=fine,
        in_specs=(tokens,) + (state,) * 7 + (stacked, stacked),
        out_specs=(tokens, stacked, stacked) + (state,) * 6,
        check_vma=False,
    )
```

time: 259 us -> 146 us (0.56)
  the two profiles are of different devices: /device:TPU:2 before, /device:TPU:24 now
where the time goes in v2:
time: 146 us; the launch traced here: 145 us
  waiting for transfers between devices  46.1 us (32%)
  starting transfers between devices  45.8 us (31%)
  between operations  14.4 us (10%)
  local copies, waits for them, and re-layouts  11.2 us (8%)
  other arithmetic  10.9 us (7%)
  blocking collectives  10.5 us (7%)
  matrix products  5.79 us (4%)
    all_to_all x1, waiting for transfers between devices, local(): lax.all_to_all(jnp.broadcast_to(shard[None], (many, EXT, 128)), group, 0,...  35 us
    all_to_all x1, starting transfers between devices, local(): lax.all_to_all(jnp.broadcast_to(shard[None], (many, EXT, 128)), group, 0,...  17.5 us
    psum x1, blocking collectives, local(): squares, cross = lax.psum(sums, 'x')  10.5 us
    ppermute x3, starting transfers between devices, exchange_x(): lax.ppermute(block_for(d), 'x', [(i, (i + d) % NX) for i in range(NX)])  9.87 us
    ppermute x1, waiting for transfers between devices, local(): packed = lax.ppermute(packed, 'yh', SWAP)  9.06 us
    all_to_all x1, starting transfers between devices, local(): arrived = lax.all_to_all(prev, ('z', 'yl', 'c'), 0, 0, tiled=True)  7.11 us
    ppermute x1, starting transfers between devices, local(): packed = lax.ppermute(packed, 'yh', SWAP)  5.02 us
    ppermute x1, starting transfers between devices, local(): got = lax.ppermute(jnp.where(yh == 0, give[1], give[0]), 'yh', SWAP)  4.37 us
  transfers between devices with their start and end apart: 10, of which 3 were waited for; matrix products, arithmetic and copies ran while one was open for 14% of the time, Pallas kernels for 0%

profile of v2, /device:TPU:24, one launch (start us, length us, event | category | flops | bytes accessed | tf_op | source)
XLA Modules:
  0.0 144.7 jit_solution(5916528879986333425)
XLA Ops:
  7.2 1.0 constant_dynamic-update-slice_fusion.4
  8.1 0.7 constant_dynamic-update-slice_fusion.3
  8.9 0.7 constant_dynamic-update-slice_fusion.2
  9.6 0.7 constant_dynamic-update-slice_fusion.1
  10.3 0.7 constant_dynamic-update-slice_fusion
  11.0 5.0 %collective-permute-start = (bf16[24,5632]{1,0:T(8,128)(2,1)S(1)}, bf16[24,5632]{1,0:T(8,128)(2,1)S(1)}, u32[]{:S(2)}, u32[]{:S(2)}) collective-permute-start(bf16[24,5632]{1,0:T(8,128)(2,1)S(1)} %constant_dynamic-update-slice_fusion), channel_id=1, source_target_pairs={{0,1},{1,0},{2,3},{3,2},{4,5},{5,4},{6,7},{7,6},{8,9},{9,8},{10,11... | collective-permute-start | bytes 811016 | tf_op jit(solution)/shard_map/ppermute | solution.py:87
  16.0 0.7 fusion.25
  18.6 0.8 convert_element_type.210
  19.4 1.4 fusion.17
  20.8 9.1 %collective-permute-done = bf16[24,5632]{1,0:T(8,128)(2,1)S(1)} collective-permute-done((bf16[24,5632]{1,0:T(8,128)(2,1)S(1)}, bf16[24,5632]{1,0:T(8,128)(2,1)S(1)}, u32[]{:S(2)}, u32[]{:S(2)}) %collective-permute-start) | collective-permute-done | bytes 270368 | tf_op jit(solution)/shard_map/ppermute | solution.py:87
  29.8 1.3 broadcast_in_dim.87
  31.1 17.5 %all-to-all-start = ((bf16[64,88,128]{2,1,0:T(8,128)(2,1)}), bf16[64,88,128]{2,1,0:T(8,128)(2,1)S(1)}, u32[]{:S(2)}, u32[]{:S(2)}) async-start(bf16[64,88,128]{2,1,0:T(8,128)(2,1)} %broadcast_in_dim.87), calls=%async_computation | async-start | bytes 2883584 | tf_op jit(solution)/shard_map/all_to_all | solution.py:102
  48.6 0.7 pad.8
  49.5 35.0 %all-to-all-done = bf16[64,88,128]{2,1,0:T(8,128)(2,1)S(1)} async-done(((bf16[64,88,128]{2,1,0:T(8,128)(2,1)}), bf16[64,88,128]{2,1,0:T(8,128)(2,1)S(1)}, u32[]{:S(2)}, u32[]{:S(2)}) %all-to-all-start) | async-done | bytes 1441824 | tf_op jit(solution)/shard_map/all_to_all | solution.py:102
  84.5 1.9 %collective-permute-start.1 = (bf16[64,88,128]{2,1,0:T(8,128)(2,1)S(1)}, bf16[64,88,128]{2,1,0:T(8,128)(2,1)}, u32[]{:S(2)}, u32[]{:S(2)}) collective-permute-start(bf16[64,88,128]{2,1,0:T(8,128)(2,1)S(1)} %all-to-all-done), channel_id=1, source_target_pairs={{0,8},{8,0},{1,9},{9,1},{2,10},{10,2},{3,11},{11,3},{4,12},{12,4},... | collective-permute-start | bytes 4325384 | tf_op jit(solution)/shard_map/ppermute | solution.py:113
  86.5 0.8 pad.7
  87.3 1.3 slice.100
  88.6 7.1 %all-to-all-start.1 = ((bf16[64,80,128]{2,1,0:T(8,128)(2,1)}), bf16[64,80,128]{2,1,0:T(8,128)(2,1)}, u32[]{:S(2)}, u32[]{:S(2)}) async-start(bf16[64,80,128]{2,1,0:T(8,128)(2,1)} %bitcast.142), calls=%async_computation.1 | async-start | bytes 2621440 | tf_op jit(solution)/shard_map/all_to_all | solution.py:111
  95.7 2.3 %fusion.3 = bf16[2,8,4,2,88,128]{5,4,2,0,1,3:T(8,128)(2,1)S(1)} fusion(bf16[1,8,2,4,88,128]{5,4,3,2,1,0:T(8,128)(2,1)} %bitcast.13, bf16[1,8,2,4,88,128]{5,4,3,2,1,0:T(8,128)(2,1)S(1)} %bitcast.138, pred[]{:T(512)S(6)} %eq.70), kind=kLoop, calls=%fused_computation.6 | loop fusion | flops 4325376 | bytes 5767169 | tf_op jit(solution)/shard_map/transpose | solution.py:115
  99.7 10.5 %psum.7 = f32[2,96]{1,0:T(2,128)S(1)} all-reduce(f32[2,96]{1,0:T(2,128)S(1)} %pad_maximum_fusion.1), channel_id=1, replica_groups=mesh['z'=8,'yl'=4,'c'=2,'x'=4,'yh'=2] {'x'}, use_global_device_ids=true, to_apply=%region_5.6 | all-reduce | flops 192 | bytes 1536 | tf_op jit(solution)/shard_map/psum | solution.py:132
  110.9 0.8 copy-done.1
  112.2 2.8 %collective-permute-start.3 = (bf16[24,5120]{1,0:T(8,128)(2,1)S(1)}, bf16[24,5120]{1,0:T(8,128)(2,1)S(1)}, u32[]{:S(2)}, u32[]{:S(2)}) collective-permute-start(bf16[24,5120]{1,0:T(8,128)(2,1)S(1)} %get-tuple-element.39), channel_id=1, source_target_pairs={{0,4},{2,6},{4,0},{6,2},{1,5},{3,7},{5,1},{7,3},{8,12},{10,14},{12... | collective-permute-start | bytes 737288 | tf_op jit(solution)/shard_map/ppermute | solution.py:60
  115.1 1.9 %collective-permute-start.4 = (bf16[24,5120]{1,0:T(8,128)(2,1)S(1)}, bf16[24,5120]{1,0:T(8,128)(2,1)S(1)}, u32[]{:S(2)}, u32[]{:S(2)}) collective-permute-start(bf16[24,5120]{1,0:T(8,128)(2,1)S(1)} %get-tuple-element.41), channel_id=1, source_target_pairs={{0,2},{2,4},{4,6},{6,0},{1,3},{3,5},{5,7},{7,1},{8,10},{10,12},{12... | collective-permute-start | bytes 737288 | tf_op jit(solution)/shard_map/ppermute | solution.py:60
  117.0 5.1 %collective-permute-start.5 = (bf16[24,5120]{1,0:T(8,128)(2,1)S(1)}, bf16[24,5120]{1,0:T(8,128)(2,1)S(1)}, u32[]{:S(2)}, u32[]{:S(2)}) collective-permute-start(bf16[24,5120]{1,0:T(8,128)(2,1)S(1)} %get-tuple-element.40), channel_id=1, source_target_pairs={{0,6},{2,0},{4,2},{6,4},{1,7},{3,1},{5,3},{7,5},{8,14},{10,8},{12,... | collective-permute-start | bytes 737288 | tf_op jit(solution)/shard_map/ppermute | solution.py:60
  122.3 4.4 %collective-permute-start.2 = (bf16[104,128]{1,0:T(8,128)(2,1)S(1)}, bf16[104,128]{1,0:T(8,128)(2,1)S(1)}, u32[]{:S(2)}, u32[]{:S(2)}) collective-permute-start(bf16[104,128]{1,0:T(8,128)(2,1)S(1)} %maximum_select_fusion.2), channel_id=1, source_target_pairs={{0,1},{1,0},{2,3},{3,2},{4,5},{5,4},{6,7},{7,6},{8,9},{9,8},{10,11... | collective-permute-start | bytes 79880 | tf_op jit(solution)/shard_map/ppermute | solution.py:151
  126.7 2.1 %fusion.13 = f32[5120,128]{1,0:T(8,128)} fusion(bf16[96,5120]{1,0:T(8,128)(2,1)S(1)} %bitcast.133, s32[]{:T(128)S(6)} %select_n.102, bf16[1,96,128]{2,1,0:T(8,128)(2,1)S(1)} %bitcast.145, bf16[1,96,128]{2,1,0:T(8,128)(2,1)S(1)} %bitcast.146), kind=kOutput, calls=%fused_computation.39 | convolution fusion | flops 125841408 | bytes 3653636 | tf_op jit(solution)/shard_map/dot_general | solution.py:156
  129.5 0.8 fusion.6
  130.3 1.9 %collective-permute-done.2 = bf16[104,128]{1,0:T(8,128)(2,1)S(1)} collective-permute-done((bf16[104,128]{1,0:T(8,128)(2,1)S(1)}, bf16[104,128]{1,0:T(8,128)(2,1)S(1)}, u32[]{:S(2)}, u32[]{:S(2)}) %collective-permute-start.2) | collective-permute-done | bytes 26656 | tf_op jit(solution)/shard_map/ppermute | solution.py:151
  132.2 1.3 slice.95
  134.0 1.6 %fusion.2 = bf16[1,5120,128]{2,1,0:T(8,128)(2,1)} fusion(f32[5120,128]{1,0:T(8,128)S(1)} %copy-done.2, bf16[96,5120]{1,0:T(8,128)(2,1)S(1)} %bitcast.139, bf16[104,128]{1,0:T(8,128)(2,1)S(1)} %collective-permute-done.2), kind=kOutput, calls=%fused_computation.4 | convolution fusion | flops 127139840 | bytes 4939776 | tf_op jit(solution)/shard_map/dot_general | solution.py:157
  135.7 1.5 %convert_reduce_fusion = f32[80,128]{1,0:T(8,128)S(1)} fusion(bf16[64,80,128]{2,1,0:T(8,128)(2,1)} %all-to-all-done.1), kind=kLoop, calls=%fused_computation.7 | loop fusion | flops 1300480 | bytes 1351680 | tf_op jit(solution)/shard_map/reduce_sum | solution.py:163
  137.2 0.7 multiply_subtract_fusion
  (70 shorter events, 6.4 us)
Async XLA Ops:
  11.0 18.9 %collective-permute-start = (bf16[24,5632]{1,0:T(8,128)(2,1)S(1)}, bf16[24,5632]{1,0:T(8,128)(2,1)S(1)}, u32[]{:S(2)}, u32[]{:S(2)}) collective-permute-start(bf16[24,5632]{1,0:T(8,128)(2,1)S(1)} %constant_dynamic-update-slice_fusion), channel_id=1, source_target_pairs={{0,1},{1,0},{2,3},{3,2},{4,5},{5,4},{6,7},{7,6},{8,9},{9,8},{10,11... | collective-permute-start | bytes 811016 | tf_op jit(solution)/shard_map/ppermute | solution.py:87
  31.1 17.5 %copy-start.3 = (bf16[24,5120]{1,0:T(8,128)(2,1)S(1)}, bf16[24,5120]{1,0:T(8,128)(2,1)}, u32[]{:S(2)}) copy-start(bf16[24,5120]{1,0:T(8,128)(2,1)} %param.10) | copy-start | bytes 737284
  31.1 55.3 %copy-start.5 = (bf16[192,128]{1,0:T(8,128)(2,1)S(1)}, bf16[192,128]{1,0:T(8,128)(2,1)}, u32[]{:S(2)}) copy-start(bf16[192,128]{1,0:T(8,128)(2,1)} %param.11) | copy-start | bytes 147460
  31.1 53.4 %all-to-all-start = ((bf16[64,88,128]{2,1,0:T(8,128)(2,1)}), bf16[64,88,128]{2,1,0:T(8,128)(2,1)S(1)}, u32[]{:S(2)}, u32[]{:S(2)}) async-start(bf16[64,88,128]{2,1,0:T(8,128)(2,1)} %broadcast_in_dim.87), calls=%async_computation | async-start | bytes 2883584 | tf_op jit(solution)/shard_map/all_to_all | solution.py:102
  48.6 38.7 %all-gather.7.cloned.1.call-start = ((), (), s32[]{:S(2)}) async-start(), calls=%async_computation.3 | async-start | bytes 1638400 | tf_op jit(solution)/shard_map/all_gather | solution.py:51
  49.4 80.9 %all-gather.5.cloned.1.call-start = ((), (), s32[]{:S(2)}) async-start(), calls=%async_computation.2 | async-start | bytes 1638400 | tf_op jit(solution)/shard_map/all_gather | solution.py:51
  84.5 11.3 %collective-permute-start.1 = (bf16[64,88,128]{2,1,0:T(8,128)(2,1)S(1)}, bf16[64,88,128]{2,1,0:T(8,128)(2,1)}, u32[]{:S(2)}, u32[]{:S(2)}) collective-permute-start(bf16[64,88,128]{2,1,0:T(8,128)(2,1)S(1)} %all-to-all-done), channel_id=1, source_target_pairs={{0,8},{8,0},{1,9},{9,1},{2,10},{10,2},{3,11},{11,3},{4,12},{12,4},... | collective-permute-start | bytes 4325384 | tf_op jit(solution)/shard_map/ppermute | solution.py:113
  88.6 47.0 %all-to-all-start.1 = ((bf16[64,80,128]{2,1,0:T(8,128)(2,1)}), bf16[64,80,128]{2,1,0:T(8,128)(2,1)}, u32[]{:S(2)}, u32[]{:S(2)}) async-start(bf16[64,80,128]{2,1,0:T(8,128)(2,1)} %bitcast.142), calls=%async_computation.1 | async-start | bytes 2621440 | tf_op jit(solution)/shard_map/all_to_all | solution.py:111
  98.6 1.1 copy-start
  110.3 1.3 copy-start.1
  112.2 17.2 %collective-permute-start.3 = (bf16[24,5120]{1,0:T(8,128)(2,1)S(1)}, bf16[24,5120]{1,0:T(8,128)(2,1)S(1)}, u32[]{:S(2)}, u32[]{:S(2)}) collective-permute-start(bf16[24,5120]{1,0:T(8,128)(2,1)S(1)} %get-tuple-element.39), channel_id=1, source_target_pairs={{0,4},{2,6},{4,0},{6,2},{1,5},{3,7},{5,1},{7,3},{8,12},{10,14},{12... | collective-permute-start | bytes 737288 | tf_op jit(solution)/shard_map/ppermute | solution.py:60
  115.1 14.4 %collective-permute-start.4 = (bf16[24,5120]{1,0:T(8,128)(2,1)S(1)}, bf16[24,5120]{1,0:T(8,128)(2,1)S(1)}, u32[]{:S(2)}, u32[]{:S(2)}) collective-permute-start(bf16[24,5120]{1,0:T(8,128)(2,1)S(1)} %get-tuple-element.41), channel_id=1, source_target_pairs={{0,2},{2,4},{4,6},{6,0},{1,3},{3,5},{5,7},{7,1},{8,10},{10,12},{12... | collective-permute-start | bytes 737288 | tf_op jit(solution)/shard_map/ppermute | solution.py:60
  117.0 12.4 %collective-permute-start.5 = (bf16[24,5120]{1,0:T(8,128)(2,1)S(1)}, bf16[24,5120]{1,0:T(8,128)(2,1)S(1)}, u32[]{:S(2)}, u32[]{:S(2)}) collective-permute-start(bf16[24,5120]{1,0:T(8,128)(2,1)S(1)} %get-tuple-element.40), channel_id=1, source_target_pairs={{0,6},{2,0},{4,2},{6,4},{1,7},{3,1},{5,3},{7,5},{8,14},{10,8},{12,... | collective-permute-start | bytes 737288 | tf_op jit(solution)/shard_map/ppermute | solution.py:60
  122.3 9.9 %collective-permute-start.2 = (bf16[104,128]{1,0:T(8,128)(2,1)S(1)}, bf16[104,128]{1,0:T(8,128)(2,1)S(1)}, u32[]{:S(2)}, u32[]{:S(2)}) collective-permute-start(bf16[104,128]{1,0:T(8,128)(2,1)S(1)} %maximum_select_fusion.2), channel_id=1, source_target_pairs={{0,1},{1,0},{2,3},{3,2},{4,5},{5,4},{6,7},{7,6},{8,9},{9,8},{10,11... | collective-permute-start | bytes 79880 | tf_op jit(solution)/shard_map/ppermute | solution.py:151
  126.7 2.1 %copy-start.8 = (f32[2,1]{0,1:T(1,128)S(1)}, f32[2,1]{0,1:T(1,128)}, u32[]{:S(2)}) copy-start(f32[2,1]{0,1:T(1,128)} %param.15) | copy-start | bytes 28
  126.7 2.1 %copy-start.9 = (f32[2,1]{0,1:T(1,128)S(1)}, f32[2,1]{0,1:T(1,128)}, u32[]{:S(2)}) copy-start(f32[2,1]{0,1:T(1,128)} %param.16) | copy-start | bytes 28
  126.7 2.1 %copy-start.10 = (f32[2,1]{0,1:T(1,128)S(1)}, f32[2,1]{0,1:T(1,128)}, u32[]{:S(2)}) copy-start(f32[2,1]{0,1:T(1,128)} %param.17) | copy-start | bytes 28
  129.4 4.6 %copy-start.2 = (f32[5120,128]{1,0:T(8,128)S(1)}, f32[5120,128]{1,0:T(8,128)}, u32[]{:S(2)}) copy-start(f32[5120,128]{1,0:T(8,128)} %fusion.13) | copy-start | bytes 7864324
  134.0 3.2 %copy-start.4 = (f32[80,128]{1,0:T(8,128)S(1)}, f32[80,128]{1,0:T(8,128)}, u32[]{:S(2)}) copy-start(f32[80,128]{1,0:T(8,128)} %param.12) | copy-start | bytes 122884
  134.0 3.2 %copy-start.6 = (f32[80,128]{1,0:T(8,128)S(1)}, f32[80,128]{1,0:T(8,128)}, u32[]{:S(2)}) copy-start(f32[80,128]{1,0:T(8,128)} %param.13) | copy-start | bytes 122884
  134.0 3.2 %copy-start.7 = (f32[80,128]{1,0:T(8,128)S(1)}, f32[80,128]{1,0:T(8,128)}, u32[]{:S(2)}) copy-start(f32[80,128]{1,0:T(8,128)} %param.14) | copy-start | bytes 122884
Sparse Core Ops, SparseCore 0:
  52.1 30.9 all-gather.6
  87.4 29.0 all-gather.4

commit v3 on v2

--- a/solution.py
+++ b/solution.py
@@ -1,6 +1,8 @@
 import jax
 import jax.numpy as jnp
 from jax import lax
+from jax.experimental import pallas as pl
+from jax.experimental.pallas import tpu as pltpu
 from jax.sharding import Mesh, PartitionSpec as P
 
 HEAD_WIDTH = 128
@@ -47,12 +49,19 @@
     return jnp.where(index == 1, hi, rest)
 
 
-def gather_x(block):
-    return lax.all_gather(jnp.pad(block, ((0, 8), (0, 0))), "x", axis=0)
-
-
-def used_rows(gathered, own):
-    return gathered[:, :own].reshape(-1, gathered.shape[2])
+def prepare(place_ref, gain_ref, prior_ref, weight_ref, out_ref):
+    lane = lax.broadcasted_iota(jnp.int32, (EXT - ROWS, 128), 1)
+    row = lax.broadcasted_iota(jnp.int32, (EXT - ROWS, 128), 0)
+    at = 2 * place_ref[0]
+    gains = jnp.where(lane == at, gain_ref[0, 0], jnp.where(lane == at + 1, gain_ref[1, 0], 0.0))
+    prior = jnp.broadcast_to(prior_ref[...], lane.shape)
+    hi = prior.astype(bf16).astype(f32)
+    mid = (prior - hi).astype(bf16).astype(f32)
+    low = prior - hi - mid
+    extra = jnp.where(row == 1, hi, jnp.where(row == 2, mid, jnp.where(row == 3, low, 0.0)))
+    extra = jnp.where(row == 0, gains, extra)
+    block = jnp.concatenate([weight_ref[...], extra], axis=0).astype(bf16)
+    out_ref[...] = jnp.broadcast_to(block[None], out_ref.shape)
 
 
 def exchange_x(block_for, mine):
@@ -81,30 +90,32 @@
     own, width = token_features.shape
     half = NX * own
 
-    cot = key_cotangent.reshape(NX, NYH, own, 128)
-    give_cot = pick(cot, 1 - yh, 1)
-    packed = jnp.concatenate([token_features] + [give_cot[i] for i in range(NX)], axis=1)
-    packed = lax.ppermute(packed, "yh", SWAP)
-    partner = packed[:, :width]
-    cot_got = packed[:, width:].reshape(own, NX, 128).transpose(1, 0, 2)
+    partner = lax.ppermute(token_features, "yh", SWAP)
 
-    place = lax.broadcasted_iota(jnp.int32, (EXT - ROWS, 128), 1)
-    first = lax.broadcasted_iota(jnp.int32, (EXT - ROWS, 128), 0) == 0
-    two = gain_master_copy.astype(bf16)
-    zero = jnp.zeros((), bf16)
-    gain_row = jnp.where(first & (place == 2 * dp), two[0, 0], zero)
-    gain_row = jnp.where(first & (place == 2 * dp + 1), two[1, 0], gain_row)
-    gain_row = gain_row + split3(prior_gain_gradient.reshape(1, 128), EXT - ROWS)
-    shard = jnp.concatenate([weight_master.astype(bf16), gain_row], axis=0)
-    shard, packed = lax.optimization_barrier((shard, packed))
     group = ("z", "yh", "yl")
     many = NZ * NYH * NYL
-    gathered = lax.all_to_all(
-        jnp.broadcast_to(shard[None], (many, EXT, 128)), group, 0, 0, tiled=True
-    )
+    shards = pl.pallas_call(
+        prepare,
+        out_shape=jax.ShapeDtypeStruct((many, EXT, 128), bf16),
+        in_specs=[
+            pl.BlockSpec(memory_space=pltpu.SMEM),
+            pl.BlockSpec(memory_space=pltpu.SMEM),
+            pl.BlockSpec(memory_space=pltpu.VMEM),
+            pl.BlockSpec(memory_space=pltpu.VMEM),
+        ],
+        out_specs=pl.BlockSpec(memory_space=pltpu.VMEM),
+        compiler_params=pltpu.CompilerParams(vmem_limit_bytes=16 * 1024 * 1024),
+    )(dp.reshape(1), gain_master_copy, prior_gain_gradient.reshape(1, 128), weight_master)
+    shards, partner = lax.optimization_barrier((shards, partner))
+    gathered = lax.all_to_all(shards, group, 0, 0, tiled=True)
 
-    rows = used_rows(gather_x(token_features), own)
-    rows_partner = gather_x(partner)
+    rows = jnp.concatenate([token_features, partner], axis=0)
+    rows = lax.all_gather(rows, "x", axis=0, tiled=True)
+
+    cot = key_cotangent.reshape(NX, NYH, own, 128)
+    cot_got = lax.ppermute(pick(cot, 1 - yh, 1), "yh", SWAP)
+    gathered, cot_got = lax.optimization_barrier((gathered, cot_got))
+    cot_two = ordered(pick(cot, yh, 1), cot_got, yh).reshape(NYH, half, 128).astype(f32)
 
     prev = weight_grad_prev.reshape(NZ * NYL * NC, ROWS, 128)
     prev, gathered = lax.optimization_barrier((prev, gathered))
@@ -118,10 +129,8 @@
     gain_two = extra[:, 0]
     summed_g = jnp.sum(pick(extra, yh, 0)[1:4], axis=0)
 
-    cot_two = ordered(pick(cot, yh, 1), cot_got, yh).reshape(NYH, half, 128).astype(f32)
-
-
     keys = [jnp.dot(rows, weight_two[h], preferred_element_type=f32) for h in range(NYH)]
+    keys = [k.reshape(NX, NYH, own, 128)[:, 0].reshape(half, 128) for k in keys]
     scaled = [cot_two[h] * gain_two[h] for h in range(NYH)]
     sums = jnp.stack(
         [
@@ -149,12 +158,11 @@
         [both_grads[1], split3(gain_terms[1:2], 8)]
     )
     got = lax.ppermute(jnp.where(yh == 0, give[1], give[0]), "yh", SWAP)
-    rows_partner, got, input_grad = lax.optimization_barrier((rows_partner, got, input_grad))
-    rows_partner = used_rows(rows_partner, own)
-    contract = (((0,), (0,)), ((), ()))
-    weight_grad = (
-        lax.dot_general(rows, pick(both_grads, yh, 0), contract, preferred_element_type=f32)
-        + lax.dot_general(rows_partner, got[:half], contract, preferred_element_type=f32)
+    got, input_grad = lax.optimization_barrier((got, input_grad))
+    kept = pick(both_grads, yh, 0).reshape(NX, 1, own, 128)
+    group_grad = jnp.concatenate([kept, got[:half].reshape(NX, 1, own, 128)], axis=1)
+    weight_grad = lax.dot_general(
+        rows, group_grad.reshape(-1, 128), (((0,), (0,)), ((), ())), preferred_element_type=f32
     ).astype(bf16)[None]
     gain_partner = jnp.sum(got[half:].astype(f32), axis=0)
     gain_grad = (pick(gain_terms, yh, 0) + gain_partner).reshape(1, 128, 1)

time: 146 us -> 138 us (0.945)
  the two profiles are of different devices: /device:TPU:24 before, /device:TPU:16 now
where the time goes in v3:
time: 138 us; the launch traced here: 137 us
  starting transfers between devices  52.4 us (38%)
  waiting for transfers between devices  41.1 us (30%)
  between operations  14.5 us (11%)
  blocking collectives  10.5 us (8%)
  other arithmetic  6.36 us (5%)
  matrix products  5.97 us (4%)
  local copies, waits for them, and re-layouts  4.69 us (3%)
  Pallas kernels  1.75 us (1%)
    ppermute x1, waiting for transfers between devices, local(): cot_got = lax.ppermute(pick(cot, 1 - yh, 1), 'yh', SWAP)  25.7 us
    all_to_all x1, starting transfers between devices, local(): gathered = lax.all_to_all(shards, group, 0, 0, tiled=True)  17.6 us
    psum x1, blocking collectives, local(): squares, cross = lax.psum(sums, 'x')  10.5 us
    ppermute x3, starting transfers between devices, exchange_x(): lax.ppermute(block_for(d), 'x', [(i, (i + d) % NX) for i in range(NX)])  9.95 us
    ppermute x1, waiting for transfers between devices, local(): partner = lax.ppermute(token_features, 'yh', SWAP)  8 us
    all_to_all x1, starting transfers between devices, local(): arrived = lax.all_to_all(prev, ('z', 'yl', 'c'), 0, 0, tiled=True)  7.24 us
    ppermute x1, starting transfers between devices, local(): partner = lax.ppermute(token_features, 'yh', SWAP)  5.94 us
    ppermute x1, starting transfers between devices, local(): cot_got = lax.ppermute(pick(cot, 1 - yh, 1), 'yh', SWAP)  5.48 us
  transfers between devices with their start and end apart: 10, of which 5 were waited for; matrix products, arithmetic and copies ran while one was open for 10% of the time, Pallas kernels for 1%

profile of v3, /device:TPU:16, one launch (start us, length us, event | category | flops | bytes accessed | tf_op | source)
XLA Modules:
  0.0 137.2 jit_solution(17670381017948837717)
XLA Ops:
  7.2 5.9 %collective-permute-start = (bf16[24,5120]{1,0:T(8,128)(2,1)}, bf16[24,5120]{1,0:T(8,128)(2,1)S(1)}, u32[]{:S(2)}, u32[]{:S(2)}) collective-permute-start(bf16[24,5120]{1,0:T(8,128)(2,1)} %param.10), channel_id=1, source_target_pairs={{0,1},{1,0},{2,3},{3,2},{4,5},{5,4},{6,7},{7,6},{8,9},{9,8},{10,11... | collective-permute-start | bytes 737288 | tf_op jit(solution)/shard_map/ppermute | solution.py:93
  13.1 0.7 copy.22.gain_ref
  13.9 0.8 copy-done
  14.7 0.7 copy-done.2
  15.3 1.8 %shard_map.169 = bf16[64,88,128]{2,1,0:T(8,128)(2,1)} custom-call(s32[1]{0:T(128)} %bitcast.1.place_ref, f32[2,1]{1,0:T(2,128)S(1)} %copy.22.gain_ref, f32[1,128]{1,0:T(1,128)S(1)} %bitcast.118, f32[80,128]{1,0:T(8,128)S(1)} %copy-done), custom_call_target="tpu_custom_call" | custom-call | tf_op jit(solution)/shard_map/pallas_call | solution.py:97
  17.1 8.0 %collective-permute-done = bf16[24,5120]{1,0:T(8,128)(2,1)S(1)} collective-permute-done((bf16[24,5120]{1,0:T(8,128)(2,1)}, bf16[24,5120]{1,0:T(8,128)(2,1)S(1)}, u32[]{:S(2)}, u32[]{:S(2)}) %collective-permute-start) | collective-permute-done | bytes 245792 | tf_op jit(solution)/shard_map/ppermute | solution.py:93
  25.1 17.6 %all-to-all-start = ((bf16[64,88,128]{2,1,0:T(8,128)(2,1)}), bf16[64,88,128]{2,1,0:T(8,128)(2,1)S(1)}, u32[]{:S(2)}, u32[]{:S(2)}) async-start(bf16[64,88,128]{2,1,0:T(8,128)(2,1)} %shard_map.169), calls=%async_computation | async-start | bytes 2883584 | tf_op jit(solution)/shard_map/all_to_all | solution.py:110
  42.7 0.8 pad_maximum_fusion
  43.6 5.5 %collective-permute-start.1 = (bf16[4,24,128]{2,1,0:T(8,128)(2,1)S(1)}, bf16[4,24,128]{2,1,0:T(8,128)(2,1)S(1)}, u32[]{:S(2)}, u32[]{:S(2)}) collective-permute-start(bf16[4,24,128]{2,1,0:T(8,128)(2,1)S(1)} %get-tuple-element.53), channel_id=1, source_target_pairs={{0,1},{1,0},{2,3},{3,2},{4,5},{5,4},{6,7},{7,6},{8,9},{9,8},{10,11... | collective-permute-start | bytes 73736 | tf_op jit(solution)/shard_map/ppermute | solution.py:116
  49.1 25.7 %collective-permute-done.1 = bf16[4,24,128]{2,1,0:T(8,128)(2,1)S(1)} collective-permute-done((bf16[4,24,128]{2,1,0:T(8,128)(2,1)S(1)}, bf16[4,24,128]{2,1,0:T(8,128)(2,1)S(1)}, u32[]{:S(2)}, u32[]{:S(2)}) %collective-permute-start.1) | collective-permute-done | bytes 24608 | tf_op jit(solution)/shard_map/ppermute | solution.py:116
  74.8 3.3 %all-to-all-done = bf16[64,88,128]{2,1,0:T(8,128)(2,1)S(1)} async-done(((bf16[64,88,128]{2,1,0:T(8,128)(2,1)}), bf16[64,88,128]{2,1,0:T(8,128)(2,1)S(1)}, u32[]{:S(2)}, u32[]{:S(2)}) %all-to-all-start) | async-done | bytes 1441824 | tf_op jit(solution)/shard_map/all_to_all | solution.py:110
  78.1 1.9 %collective-permute-start.2 = (bf16[64,88,128]{2,1,0:T(8,128)(2,1)S(1)}, bf16[64,88,128]{2,1,0:T(8,128)(2,1)}, u32[]{:S(2)}, u32[]{:S(2)}) collective-permute-start(bf16[64,88,128]{2,1,0:T(8,128)(2,1)S(1)} %all-to-all-done), channel_id=1, source_target_pairs={{0,8},{8,0},{1,9},{9,1},{2,10},{10,2},{3,11},{11,3},{4,12},{12,4},... | collective-permute-start | bytes 4325384 | tf_op jit(solution)/shard_map/ppermute | solution.py:124
  80.1 7.2 %all-to-all-start.1 = ((bf16[64,80,128]{2,1,0:T(8,128)(2,1)}), bf16[64,80,128]{2,1,0:T(8,128)(2,1)S(1)}, u32[]{:S(2)}, u32[]{:S(2)}) async-start(bf16[64,80,128]{2,1,0:T(8,128)(2,1)} %bitcast.128), calls=%async_computation.1 | async-start | bytes 2621440 | tf_op jit(solution)/shard_map/all_to_all | solution.py:122
  87.4 2.2 %fusion.2 = bf16[2,8,4,2,88,128]{5,4,2,0,1,3:T(8,128)(2,1)S(1)} fusion(bf16[1,8,2,4,88,128]{5,4,3,2,1,0:T(8,128)(2,1)} %bitcast.7, bf16[1,8,2,4,88,128]{5,4,3,2,1,0:T(8,128)(2,1)S(1)} %bitcast.119, pred[]{:T(512)S(6)} %eq.29), kind=kLoop, calls=%fused_computation.5 | loop fusion | flops 4325376 | bytes 5767169 | tf_op jit(solution)/shard_map/transpose | solution.py:126
  89.8 1.2 copy.24
  91.2 2.3 %multiply_reduce_fusion.2 = (f32[4,24]{1,0:T(4,128)S(1)}, f32[4,24]{1,0:T(4,128)S(1)}, f32[4,1,24,128]{3,2,1,0:T(8,128)S(1)}) fusion(f32[4,1,24,128]{3,2,1,0:T(8,128)S(1)} %bitcast.137, f32[128]{0:T(128)S(1)} %get-tuple-element.54, bf16[4,2,24,5120]{3,2,1,0:T(8,128)(2,1)} %bitcast.126, bf16[5120,128,1,1]{1,0,3,2:T(8,128)(2,1)} %bitcast.122), kind=kOutput, calls=%fused_computation.40 | convolution fusion | flops 125890368 | bytes 3376384 | tf_op jit(solution)/shard_map/slice | solution.py:133
  93.5 0.6 multiply_reduce_fusion.3
  94.3 10.5 %psum.7 = f32[2,96]{1,0:T(2,128)S(1)} all-reduce(f32[2,96]{1,0:T(2,128)S(1)} %pad_maximum_fusion.2), channel_id=1, replica_groups=mesh['z'=8,'yl'=4,'c'=2,'x'=4,'yh'=2] {'x'}, use_global_device_ids=true, to_apply=%region_5.6 | all-reduce | flops 192 | bytes 1536 | tf_op jit(solution)/shard_map/psum | solution.py:141
  105.0 0.6 fusion.18
  105.6 0.8 copy-done.3
  106.3 0.6 fusion
  107.0 2.9 %collective-permute-start.4 = (bf16[24,5120]{1,0:T(8,128)(2,1)S(1)}, bf16[24,5120]{1,0:T(8,128)(2,1)S(1)}, u32[]{:S(2)}, u32[]{:S(2)}) collective-permute-start(bf16[24,5120]{1,0:T(8,128)(2,1)S(1)} %get-tuple-element.43), channel_id=1, source_target_pairs={{0,4},{2,6},{4,0},{6,2},{1,5},{3,7},{5,1},{7,3},{8,12},{10,14},{12... | collective-permute-start | bytes 737288 | tf_op jit(solution)/shard_map/ppermute | solution.py:69
  109.9 1.9 %collective-permute-start.5 = (bf16[24,5120]{1,0:T(8,128)(2,1)S(1)}, bf16[24,5120]{1,0:T(8,128)(2,1)S(1)}, u32[]{:S(2)}, u32[]{:S(2)}) collective-permute-start(bf16[24,5120]{1,0:T(8,128)(2,1)S(1)} %get-tuple-element.45), channel_id=1, source_target_pairs={{0,2},{2,4},{4,6},{6,0},{1,3},{3,5},{5,7},{7,1},{8,10},{10,12},{12... | collective-permute-start | bytes 737288 | tf_op jit(solution)/shard_map/ppermute | solution.py:69
  111.8 5.1 %collective-permute-start.6 = (bf16[24,5120]{1,0:T(8,128)(2,1)S(1)}, bf16[24,5120]{1,0:T(8,128)(2,1)S(1)}, u32[]{:S(2)}, u32[]{:S(2)}) collective-permute-start(bf16[24,5120]{1,0:T(8,128)(2,1)S(1)} %get-tuple-element.44), channel_id=1, source_target_pairs={{0,6},{2,0},{4,2},{6,4},{1,7},{3,1},{5,3},{7,5},{8,14},{10,8},{12,... | collective-permute-start | bytes 737288 | tf_op jit(solution)/shard_map/ppermute | solution.py:69
  117.1 4.2 %collective-permute-start.3 = (bf16[104,128]{1,0:T(8,128)(2,1)S(1)}, bf16[104,128]{1,0:T(8,128)(2,1)S(1)}, u32[]{:S(2)}, u32[]{:S(2)}) collective-permute-start(bf16[104,128]{1,0:T(8,128)(2,1)S(1)} %maximum_select_fusion.2), channel_id=1, source_target_pairs={{0,1},{1,0},{2,3},{3,2},{4,5},{5,4},{6,7},{7,6},{8,9},{9,8},{10,11... | collective-permute-start | bytes 79880 | tf_op jit(solution)/shard_map/ppermute | solution.py:160
  121.4 0.6 multiply_subtract_fusion.1
  122.0 0.3 collective-permute-done.5
  122.4 0.8 fusion.5
  123.2 3.7 %collective-permute-done.3 = bf16[104,128]{1,0:T(8,128)(2,1)S(1)} collective-permute-done((bf16[104,128]{1,0:T(8,128)(2,1)S(1)}, bf16[104,128]{1,0:T(8,128)(2,1)S(1)}, u32[]{:S(2)}, u32[]{:S(2)}) %collective-permute-start.3) | collective-permute-done | bytes 26656 | tf_op jit(solution)/shard_map/ppermute | solution.py:160
  127.0 2.0 %fusion.1 = bf16[1,5120,128]{2,1,0:T(8,128)(2,1)} fusion(bf16[192,5120]{1,0:T(8,128)(2,1)S(1)} %copy-done.5, bf16[192,128]{1,0:T(8,128)(2,1)S(1)} %bitcast.131), kind=kOutput, calls=%fused_computation.3 | convolution fusion | flops 252313600 | bytes 3325952 | tf_op jit(solution)/shard_map/dot_general | solution.py:164
  129.0 0.5 fusion.23
  129.7 0.7 multiply_subtract_fusion
  (60 shorter events, 1.4 us)
Async XLA Ops:
  7.2 17.9 %collective-permute-start = (bf16[24,5120]{1,0:T(8,128)(2,1)}, bf16[24,5120]{1,0:T(8,128)(2,1)S(1)}, u32[]{:S(2)}, u32[]{:S(2)}) collective-permute-start(bf16[24,5120]{1,0:T(8,128)(2,1)} %param.10), channel_id=1, source_target_pairs={{0,1},{1,0},{2,3},{3,2},{4,5},{5,4},{6,7},{7,6},{8,9},{9,8},{10,11... | collective-permute-start | bytes 737288 | tf_op jit(solution)/shard_map/ppermute | solution.py:93
  13.9 0.8 copy-start
  14.7 0.7 copy-start.2
  17.1 25.7 %copy-start.6 = (bf16[24,5120]{1,0:T(8,128)(2,1)S(1)}, bf16[24,5120]{1,0:T(8,128)(2,1)}, u32[]{:S(2)}) copy-start(bf16[24,5120]{1,0:T(8,128)(2,1)} %param.10) | copy-start | bytes 737284
  25.1 53.1 %all-to-all-start = ((bf16[64,88,128]{2,1,0:T(8,128)(2,1)}), bf16[64,88,128]{2,1,0:T(8,128)(2,1)S(1)}, u32[]{:S(2)}, u32[]{:S(2)}) async-start(bf16[64,88,128]{2,1,0:T(8,128)(2,1)} %shard_map.169), calls=%async_computation | async-start | bytes 2883584 | tf_op jit(solution)/shard_map/all_to_all | solution.py:110
  42.7 0.9 copy-start.7
  42.7 48.5 %all-gather.2.cloned.1.call-start = ((), (), s32[]{:S(2)}) async-start(), calls=%async_computation.2 | async-start | bytes 2457600 | tf_op jit(solution)/shard_map/all_gather | solution.py:113
  43.6 31.2 %collective-permute-start.1 = (bf16[4,24,128]{2,1,0:T(8,128)(2,1)S(1)}, bf16[4,24,128]{2,1,0:T(8,128)(2,1)S(1)}, u32[]{:S(2)}, u32[]{:S(2)}) collective-permute-start(bf16[4,24,128]{2,1,0:T(8,128)(2,1)S(1)} %get-tuple-element.53), channel_id=1, source_target_pairs={{0,1},{1,0},{2,3},{3,2},{4,5},{5,4},{6,7},{7,6},{8,9},{9,8},{10,11... | collective-permute-start | bytes 73736 | tf_op jit(solution)/shard_map/ppermute | solution.py:116
  78.1 9.3 %collective-permute-start.2 = (bf16[64,88,128]{2,1,0:T(8,128)(2,1)S(1)}, bf16[64,88,128]{2,1,0:T(8,128)(2,1)}, u32[]{:S(2)}, u32[]{:S(2)}) collective-permute-start(bf16[64,88,128]{2,1,0:T(8,128)(2,1)S(1)} %all-to-all-done), channel_id=1, source_target_pairs={{0,8},{8,0},{1,9},{9,1},{2,10},{10,2},{3,11},{11,3},{4,12},{12,4},... | collective-permute-start | bytes 4325384 | tf_op jit(solution)/shard_map/ppermute | solution.py:124
  80.1 49.4 %all-to-all-start.1 = ((bf16[64,80,128]{2,1,0:T(8,128)(2,1)}), bf16[64,80,128]{2,1,0:T(8,128)(2,1)S(1)}, u32[]{:S(2)}, u32[]{:S(2)}) async-start(bf16[64,80,128]{2,1,0:T(8,128)(2,1)} %bitcast.128), calls=%async_computation.1 | async-start | bytes 2621440 | tf_op jit(solution)/shard_map/all_to_all | solution.py:122
  91.2 2.3 %copy-start.4 = (bf16[192,5120]{1,0:T(8,128)(2,1)S(1)}, bf16[192,5120]{1,0:T(8,128)(2,1)}, u32[]{:S(2)}) copy-start(bf16[192,5120]{1,0:T(8,128)(2,1)} %all-gather.2.cloned.1.call-done) | copy-start | bytes 5898244
  105.0 1.3 copy-start.3
  106.9 14.5 %copy-start.10 = (f32[2,1]{0,1:T(1,128)S(1)}, f32[2,1]{0,1:T(1,128)}, u32[]{:S(2)}) copy-start(f32[2,1]{0,1:T(1,128)} %param.15) | copy-start | bytes 28
  106.9 14.5 %copy-start.11 = (f32[2,1]{0,1:T(1,128)S(1)}, f32[2,1]{0,1:T(1,128)}, u32[]{:S(2)}) copy-start(f32[2,1]{0,1:T(1,128)} %param.16) | copy-start | bytes 28
  106.9 14.5 %copy-start.12 = (f32[2,1]{0,1:T(1,128)S(1)}, f32[2,1]{0,1:T(1,128)}, u32[]{:S(2)}) copy-start(f32[2,1]{0,1:T(1,128)} %param.17) | copy-start | bytes 28
  106.9 20.0 %copy-start.5 = (bf16[192,5120]{1,0:T(8,128)(2,1)S(1)}, bf16[192,5120]{1,0:T(8,128)(2,1)}, u32[]{:S(2)}) copy-start(bf16[192,5120]{1,0:T(8,128)(2,1)} %all-gather.2.cloned.1.call-done) | copy-start | bytes 5898244
  107.0 15.1 %collective-permute-start.4 = (bf16[24,5120]{1,0:T(8,128)(2,1)S(1)}, bf16[24,5120]{1,0:T(8,128)(2,1)S(1)}, u32[]{:S(2)}, u32[]{:S(2)}) collective-permute-start(bf16[24,5120]{1,0:T(8,128)(2,1)S(1)} %get-tuple-element.43), channel_id=1, source_target_pairs={{0,4},{2,6},{4,0},{6,2},{1,5},{3,7},{5,1},{7,3},{8,12},{10,14},{12... | collective-permute-start | bytes 737288 | tf_op jit(solution)/shard_map/ppermute | solution.py:69
  109.9 12.5 %collective-permute-start.5 = (bf16[24,5120]{1,0:T(8,128)(2,1)S(1)}, bf16[24,5120]{1,0:T(8,128)(2,1)S(1)}, u32[]{:S(2)}, u32[]{:S(2)}) collective-permute-start(bf16[24,5120]{1,0:T(8,128)(2,1)S(1)} %get-tuple-element.45), channel_id=1, source_target_pairs={{0,2},{2,4},{4,6},{6,0},{1,3},{3,5},{5,7},{7,1},{8,10},{10,12},{12... | collective-permute-start | bytes 737288 | tf_op jit(solution)/shard_map/ppermute | solution.py:69
  111.8 10.5 %collective-permute-start.6 = (bf16[24,5120]{1,0:T(8,128)(2,1)S(1)}, bf16[24,5120]{1,0:T(8,128)(2,1)S(1)}, u32[]{:S(2)}, u32[]{:S(2)}) collective-permute-start(bf16[24,5120]{1,0:T(8,128)(2,1)S(1)} %get-tuple-element.44), channel_id=1, source_target_pairs={{0,6},{2,0},{4,2},{6,4},{1,7},{3,1},{5,3},{7,5},{8,14},{10,8},{12,... | collective-permute-start | bytes 737288 | tf_op jit(solution)/shard_map/ppermute | solution.py:69
  117.1 9.8 %collective-permute-start.3 = (bf16[104,128]{1,0:T(8,128)(2,1)S(1)}, bf16[104,128]{1,0:T(8,128)(2,1)S(1)}, u32[]{:S(2)}, u32[]{:S(2)}) collective-permute-start(bf16[104,128]{1,0:T(8,128)(2,1)S(1)} %maximum_select_fusion.2), channel_id=1, source_target_pairs={{0,1},{1,0},{2,3},{3,2},{4,5},{5,4},{6,7},{7,6},{8,9},{9,8},{10,11... | collective-permute-start | bytes 79880 | tf_op jit(solution)/shard_map/ppermute | solution.py:160
  126.9 2.7 %copy-start.1 = (f32[80,128]{1,0:T(8,128)S(1)}, f32[80,128]{1,0:T(8,128)}, u32[]{:S(2)}) copy-start(f32[80,128]{1,0:T(8,128)} %weight_ref.1) | copy-start | bytes 122884
  127.0 2.7 %copy-start.8 = (f32[80,128]{1,0:T(8,128)S(1)}, f32[80,128]{1,0:T(8,128)}, u32[]{:S(2)}) copy-start(f32[80,128]{1,0:T(8,128)} %param.13) | copy-start | bytes 122884
  127.0 2.7 %copy-start.9 = (f32[80,128]{1,0:T(8,128)S(1)}, f32[80,128]{1,0:T(8,128)}, u32[]{:S(2)}) copy-start(f32[80,128]{1,0:T(8,128)} %param.14) | copy-start | bytes 122884
Sparse Core Ops, SparseCore 0:
  45.6 35.7 all-gather.1

commit v4 on v3

--- a/solution.py
+++ b/solution.py
@@ -20,6 +20,7 @@
 NZ, NYL, NC, NX, NYH = 8, 4, 2, 4, 2
 ROWS = 80
 EXT = 88
+AXES = ("z", "yl", "c", "x", "yh")
 SWAP = [(0, 1), (1, 0)]
 f32, bf16 = jnp.float32, jnp.bfloat16
 
@@ -47,6 +48,18 @@
     zero = jnp.zeros((), bf16)
     rest = jnp.where(index == 2, mid, jnp.where(index == 3, low, zero))
     return jnp.where(index == 1, hi, rest)
+
+
+def rings(core, z_varies):
+    def at(z, y, x):
+        return (((z * NYL + y % NYL) * NC + core) * NX + x) * NYH + y // NYL
+
+    spread, fixed = (NZ, NYH * NYL) if z_varies else (NYH * NYL, NZ)
+    return [
+        [at(i, j, x) if z_varies else at(j, i, x) for i in range(spread)]
+        for x in range(NX)
+        for j in range(fixed)
+    ]
 
 
 def prepare(place_ref, gain_ref, prior_ref, weight_ref, out_ref):
@@ -92,11 +105,10 @@
 
     partner = lax.ppermute(token_features, "yh", SWAP)
 
-    group = ("z", "yh", "yl")
-    many = NZ * NYH * NYL
+    ring = NYH * NYL
     shards = pl.pallas_call(
         prepare,
-        out_shape=jax.ShapeDtypeStruct((many, EXT, 128), bf16),
+        out_shape=jax.ShapeDtypeStruct((NZ, EXT, 128), bf16),
         in_specs=[
             pl.BlockSpec(memory_space=pltpu.SMEM),
             pl.BlockSpec(memory_space=pltpu.SMEM),
@@ -106,8 +118,15 @@
         out_specs=pl.BlockSpec(memory_space=pltpu.VMEM),
         compiler_params=pltpu.CompilerParams(vmem_limit_bytes=16 * 1024 * 1024),
     )(dp.reshape(1), gain_master_copy, prior_gain_gradient.reshape(1, 128), weight_master)
-    shards, partner = lax.optimization_barrier((shards, partner))
-    gathered = lax.all_to_all(shards, group, 0, 0, tiled=True)
+    along_z, along_y = [rings(core, True) for core in range(NC)], [rings(core, False) for core in range(NC)]
+    first = lax.all_to_all(
+        shards, AXES, 0, 0, tiled=True, axis_index_groups=along_z[0] + along_y[1]
+    )
+    first, partner = lax.optimization_barrier((first, partner))
+    gathered = lax.all_to_all(
+        jnp.broadcast_to(first.reshape(1, -1, 128), (ring, NZ * EXT, 128)),
+        AXES, 0, 0, tiled=True, axis_index_groups=along_y[0] + along_z[1],
+    )
 
     rows = jnp.concatenate([token_features, partner], axis=0)
     rows = lax.all_gather(rows, "x", axis=0, tiled=True)
@@ -117,13 +136,17 @@
     gathered, cot_got = lax.optimization_barrier((gathered, cot_got))
     cot_two = ordered(pick(cot, yh, 1), cot_got, yh).reshape(NYH, half, 128).astype(f32)
 
-    prev = weight_grad_prev.reshape(NZ * NYL * NC, ROWS, 128)
-    prev, gathered = lax.optimization_barrier((prev, gathered))
-    arrived = lax.all_to_all(prev, ("z", "yl", "c"), 0, 0, tiled=True)
+    prev = weight_grad_prev.reshape(NZ * NYL, NC, ROWS, 128)
+    other_core = lax.ppermute(pick(prev, 1 - c, 1), "c", SWAP)
+    pair = (pick(prev, c, 1).astype(f32) + other_core.astype(f32)).astype(bf16)
+    pair, gathered = lax.optimization_barrier((pair, gathered))
+    arrived = lax.all_to_all(pair, ("z", "yl"), 0, 0, tiled=True)
 
     gathered_other = lax.ppermute(gathered, "c", SWAP)
-    both = ordered(gathered, gathered_other, c).reshape(NC, NZ, NYH, NYL, EXT, 128)
-    both = both.transpose(2, 1, 3, 0, 4, 5)
+    both = ordered(gathered, gathered_other, c)
+    core_0 = both[0].reshape(NYH, NYL, NZ, EXT, 128).transpose(0, 2, 1, 3, 4)
+    core_1 = both[1].reshape(NZ, NYH, NYL, EXT, 128).transpose(1, 0, 2, 3, 4)
+    both = jnp.stack([core_0, core_1], axis=3)
     weight_two = both[:, :, :, :, :ROWS].reshape(NYH, width, 128)
     extra = jnp.sum(both[:, :, :, :, ROWS:].astype(f32), axis=(1, 2, 3))
     gain_two = extra[:, 0]
@@ -176,7 +199,7 @@
 
 
 def solution(mesh):
-    fine = Mesh(mesh.devices.reshape(NZ, NYL, NC, NX, NYH), ("z", "yl", "c", "x", "yh"))
+    fine = Mesh(mesh.devices.reshape(NZ, NYL, NC, NX, NYH), AXES)
     dp, tensor = ("z", "yl", "c"), ("x", "yh")
     state = P(dp, tensor)
     stacked = P(dp, None, tensor)

time: 138 us -> 133 us (0.964)
  the two profiles are of different devices: /device:TPU:16 before, /device:TPU:8 now
where the time goes in v4:
time: 133 us; the launch traced here: 132 us
  starting transfers between devices  66.1 us (50%)
  waiting for transfers between devices  19.9 us (15%)
  between operations  14.5 us (11%)
  other arithmetic  10.7 us (8%)
  blocking collectives  9.03 us (7%)
  matrix products  5.57 us (4%)
  local copies, waits for them, and re-layouts  5.01 us (4%)
    all_to_all x1, starting transfers between devices, local(): lax.all_to_all(shards, AXES, 0, 0, tiled=True, axis_index_groups=along_z[...  10.3 us
    all_to_all x1, starting transfers between devices, local(): arrived = lax.all_to_all(pair, ('z', 'yl'), 0, 0, tiled=True)  10.2 us
    ppermute x3, starting transfers between devices, exchange_x(): lax.ppermute(block_for(d), 'x', [(i, (i + d) % NX) for i in range(NX)])  9.95 us
    psum x1, blocking collectives, local(): squares, cross = lax.psum(sums, 'x')  9.03 us
    ppermute x1, waiting for transfers between devices, local(): partner = lax.ppermute(token_features, 'yh', SWAP)  8.39 us
    all_to_all x1, starting transfers between devices, local(): lax.all_to_all(jnp.broadcast_to(first.reshape(1, -1, 128), (ring, NZ * EX...  7.9 us
    ppermute x1, waiting for transfers between devices, local(): cot_got = lax.ppermute(pick(cot, 1 - yh, 1), 'yh', SWAP)  7.35 us
    ppermute x1, starting transfers between devices, local(): partner = lax.ppermute(token_features, 'yh', SWAP)  6.83 us
  transfers between devices with their start and end apart: 12, of which 4 were waited for; matrix products, arithmetic and copies ran while one was open for 11% of the time, Pallas kernels for 0%

profile of v4, /device:TPU:8, one launch (start us, length us, event | category | flops | bytes accessed | tf_op | source)
XLA Modules:
  0.0 132.1 jit_solution(3142381999606819549)
XLA Ops:
  7.2 0.7 copy.20.gain_ref
  7.9 0.8 copy-done
  8.7 0.7 copy-done.2
  9.4 1.2 shard_map.169
  10.6 10.3 %all-to-all-start = ((bf16[8,88,128]{2,1,0:T(8,128)(2,1)}), bf16[8,88,128]{2,1,0:T(8,128)(2,1)S(1)}, u32[]{:S(2)}, u32[]{:S(2)}) async-start(bf16[8,88,128]{2,1,0:T(8,128)(2,1)} %shard_map.169), calls=%async_computation | async-start | bytes 360448 | tf_op jit(solution)/shard_map/all_to_all | solution.py:122
  20.9 6.8 %collective-permute-start.1 = (bf16[24,5120]{1,0:T(8,128)(2,1)}, bf16[24,5120]{1,0:T(8,128)(2,1)}, u32[]{:S(2)}, u32[]{:S(2)}) collective-permute-start(bf16[24,5120]{1,0:T(8,128)(2,1)} %param.10), channel_id=1, source_target_pairs={{0,1},{1,0},{2,3},{3,2},{4,5},{5,4},{6,7},{7,6},{8,9},{9,8},{10,11... | collective-permute-start | bytes 737288 | tf_op jit(solution)/shard_map/ppermute | solution.py:106
  27.7 8.4 %collective-permute-done.1 = bf16[24,5120]{1,0:T(8,128)(2,1)} collective-permute-done((bf16[24,5120]{1,0:T(8,128)(2,1)}, bf16[24,5120]{1,0:T(8,128)(2,1)}, u32[]{:S(2)}, u32[]{:S(2)}) %collective-permute-start.1) | collective-permute-done | bytes 245792 | tf_op jit(solution)/shard_map/ppermute | solution.py:106
  36.1 1.3 broadcast_in_dim.57
  37.4 7.9 %all-to-all-start.1 = ((bf16[8,704,128]{2,1,0:T(8,128)(2,1)}), bf16[8,704,128]{2,1,0:T(8,128)(2,1)S(1)}, u32[]{:S(2)}, u32[]{:S(2)}) async-start(bf16[8,704,128]{2,1,0:T(8,128)(2,1)} %broadcast_in_dim.57), calls=%async_computation.1 | async-start | bytes 2883584 | tf_op jit(solution)/shard_map/all_to_all | solution.py:126
  45.4 4.4 %collective-permute-start = (bf16[32,80,128]{2,1,0:T(8,128)(2,1)S(1)}, bf16[32,80,128]{2,1,0:T(8,128)(2,1)}, u32[]{:S(2)}, u32[]{:S(2)}) collective-permute-start(bf16[32,80,128]{2,1,0:T(8,128)(2,1)S(1)} %dynamic-slice_bitcast_fusion), channel_id=1, source_target_pairs={{0,8},{8,0},{1,9},{9,1},{2,10},{10,2},{3,11},{11,3},{4,12},{12,4},... | collective-permute-start | bytes 1966088 | tf_op jit(solution)/shard_map/ppermute | solution.py:140
  49.9 1.9 %pad_maximum_fusion = bf16[48,5120]{1,0:T(8,128)(2,1)} fusion(bf16[24,5120]{1,0:T(8,128)(2,1)} %collective-permute-done.1, bf16[24,5120]{1,0:T(8,128)(2,1)} %param.10), kind=kLoop, calls=%fused_computation.17 | loop fusion | flops 983040 | bytes 983040 | tf_op jit(solution)/shard_map/concatenate | solution.py:131
  51.8 6.8 %collective-permute-start.2 = (bf16[4,24,128]{2,1,0:T(8,128)(2,1)S(1)}, bf16[4,24,128]{2,1,0:T(8,128)(2,1)S(1)}, u32[]{:S(2)}, u32[]{:S(2)}) collective-permute-start(bf16[4,24,128]{2,1,0:T(8,128)(2,1)S(1)} %get-tuple-element.55), channel_id=1, source_target_pairs={{0,1},{1,0},{2,3},{3,2},{4,5},{5,4},{6,7},{7,6},{8,9},{9,8},{10,11... | collective-permute-start | bytes 73736 | tf_op jit(solution)/shard_map/ppermute | solution.py:135
  58.6 2.1 %fusion.4 = bf16[32,80,128]{2,1,0:T(8,128)(2,1)} fusion(bf16[32,80,128]{2,1,0:T(8,128)(2,1)} %collective-permute-done, bf16[32,2,80,128]{3,2,1,0:T(8,128)(2,1)S(1)} %bitcast.149, s32[]{:T(128)S(6)} %select_n.81), kind=kLoop, calls=%fused_computation.13 | loop fusion | flops 1310720 | bytes 1966084 | tf_op jit(solution)/shard_map/convert_element_type | solution.py:141
  60.7 7.4 %collective-permute-done.2 = bf16[4,24,128]{2,1,0:T(8,128)(2,1)S(1)} collective-permute-done((bf16[4,24,128]{2,1,0:T(8,128)(2,1)S(1)}, bf16[4,24,128]{2,1,0:T(8,128)(2,1)S(1)}, u32[]{:S(2)}, u32[]{:S(2)}) %collective-permute-start.2) | collective-permute-done | bytes 24608 | tf_op jit(solution)/shard_map/ppermute | solution.py:135
  68.1 3.7 %collective-permute-start.3 = (bf16[8,704,128]{2,1,0:T(8,128)(2,1)S(1)}, bf16[8,704,128]{2,1,0:T(8,128)(2,1)}, u32[]{:S(2)}, u32[]{:S(2)}) collective-permute-start(bf16[8,704,128]{2,1,0:T(8,128)(2,1)S(1)} %all-to-all-done.1), channel_id=1, source_target_pairs={{0,8},{8,0},{1,9},{9,1},{2,10},{10,2},{3,11},{11,3},{4,12},{12,4},... | collective-permute-start | bytes 4325384 | tf_op jit(solution)/shard_map/ppermute | solution.py:145
  72.8 10.2 %all-to-all-start.2 = ((bf16[32,80,128]{2,1,0:T(8,128)(2,1)}), bf16[32,80,128]{2,1,0:T(8,128)(2,1)S(1)}, u32[]{:S(2)}, u32[]{:S(2)}) async-start(bf16[32,80,128]{2,1,0:T(8,128)(2,1)} %fusion.4), calls=%async_computation.2 | async-start | bytes 1310720 | tf_op jit(solution)/shard_map/all_to_all | solution.py:143
  83.0 0.6 fusion.32
  83.7 2.2 %maximum_select_fusion = bf16[2,8,704,128]{3,2,1,0:T(8,128)(2,1)S(1)} fusion(bf16[1,8,704,128]{3,2,1,0:T(8,128)(2,1)} %bitcast.10, bf16[1,8,704,128]{3,2,1,0:T(8,128)(2,1)S(1)} %bitcast.138, pred[]{:T(512)S(6)} %eq.29), kind=kLoop, calls=%fused_computation.8 | loop fusion | flops 4325376 | bytes 5767169 | tf_op jit(solution)/shard_map/jit(_where)/select_n | solution.py:40
  86.7 2.1 %all-gather.2.cloned.1.call-done = bf16[192,5120]{1,0:T(8,128)(2,1)} async-done(((bf16[48,5120]{1,0:T(8,128)(2,1)}), bf16[192,5120]{1,0:T(8,128)(2,1)}) %all-gather.2.cloned.1.call-update) | async-done | bytes 1966096 | tf_op jit(solution)/shard_map/all_gather | solution.py:132
  88.8 1.9 %multiply_reduce_fusion.2 = (f32[4,24]{1,0:T(4,128)S(1)}, f32[4,24]{1,0:T(4,128)S(1)}, f32[4,1,24,128]{3,2,1,0:T(8,128)S(1)}) fusion(f32[4,1,24,128]{3,2,1,0:T(8,128)S(1)} %bitcast.159, f32[128]{0:T(128)S(1)} %get-tuple-element.56, bf16[4,2,24,5120]{3,2,1,0:T(8,128)(2,1)} %bitcast.146, bf16[5120,128,1,1]{1,0,3,2:T(8,128)(2,1)S(1)} %bitcast.142), kind=kOutput, calls=%fused_computation.50 | convolution fusion | flops 125890368 | bytes 3376384 | tf_op jit(solution)/shard_map/slice | solution.py:156
  90.8 0.6 multiply_reduce_fusion.3
  91.5 9.0 %psum.7 = f32[2,96]{1,0:T(2,128)S(1)} all-reduce(f32[2,96]{1,0:T(2,128)S(1)} %pad_maximum_fusion.3), channel_id=1, replica_groups=mesh['z'=8,'yl'=4,'c'=2,'x'=4,'yh'=2] {'x'}, use_global_device_ids=true, to_apply=%region_5.6 | all-reduce | flops 192 | bytes 1536 | tf_op jit(solution)/shard_map/psum | solution.py:164
  101.4 0.6 fusion
  102.1 2.9 %collective-permute-start.5 = (bf16[24,5120]{1,0:T(8,128)(2,1)S(1)}, bf16[24,5120]{1,0:T(8,128)(2,1)S(1)}, u32[]{:S(2)}, u32[]{:S(2)}) collective-permute-start(bf16[24,5120]{1,0:T(8,128)(2,1)S(1)} %get-tuple-element.45), channel_id=1, source_target_pairs={{0,4},{2,6},{4,0},{6,2},{1,5},{3,7},{5,1},{7,3},{8,12},{10,14},{12... | collective-permute-start | bytes 737288 | tf_op jit(solution)/shard_map/ppermute | solution.py:82
  105.0 2.6 %collective-permute-start.6 = (bf16[24,5120]{1,0:T(8,128)(2,1)S(1)}, bf16[24,5120]{1,0:T(8,128)(2,1)S(1)}, u32[]{:S(2)}, u32[]{:S(2)}) collective-permute-start(bf16[24,5120]{1,0:T(8,128)(2,1)S(1)} %get-tuple-element.47), channel_id=1, source_target_pairs={{0,2},{2,4},{4,6},{6,0},{1,3},{3,5},{5,7},{7,1},{8,10},{10,12},{12... | collective-permute-start | bytes 737288 | tf_op jit(solution)/shard_map/ppermute | solution.py:82
  107.7 4.4 %collective-permute-start.7 = (bf16[24,5120]{1,0:T(8,128)(2,1)S(1)}, bf16[24,5120]{1,0:T(8,128)(2,1)S(1)}, u32[]{:S(2)}, u32[]{:S(2)}) collective-permute-start(bf16[24,5120]{1,0:T(8,128)(2,1)S(1)} %get-tuple-element.46), channel_id=1, source_target_pairs={{0,6},{2,0},{4,2},{6,4},{1,7},{3,1},{5,3},{7,5},{8,14},{10,8},{12,... | collective-permute-start | bytes 737288 | tf_op jit(solution)/shard_map/ppermute | solution.py:82
  112.2 6.0 %collective-permute-start.4 = (bf16[104,128]{1,0:T(8,128)(2,1)S(1)}, bf16[104,128]{1,0:T(8,128)(2,1)S(1)}, u32[]{:S(2)}, u32[]{:S(2)}) collective-permute-start(bf16[104,128]{1,0:T(8,128)(2,1)S(1)} %maximum_select_fusion.2), channel_id=1, source_target_pairs={{0,1},{1,0},{2,3},{3,2},{4,5},{5,4},{6,7},{7,6},{8,9},{9,8},{10,11... | collective-permute-start | bytes 79880 | tf_op jit(solution)/shard_map/ppermute | solution.py:183
  118.3 0.6 multiply_subtract_fusion.1
  119.0 0.8 fusion.7
  119.8 2.1 %collective-permute-done.4 = bf16[104,128]{1,0:T(8,128)(2,1)S(1)} collective-permute-done((bf16[104,128]{1,0:T(8,128)(2,1)S(1)}, bf16[104,128]{1,0:T(8,128)(2,1)S(1)}, u32[]{:S(2)}, u32[]{:S(2)}) %collective-permute-start.4) | collective-permute-done | bytes 26656 | tf_op jit(solution)/shard_map/ppermute | solution.py:183
  122.6 0.7 multiply_subtract_fusion
  123.2 2.0 %fusion.1 = bf16[1,5120,128]{2,1,0:T(8,128)(2,1)} fusion(bf16[192,5120]{1,0:T(8,128)(2,1)S(1)} %copy-done.4, bf16[192,128]{1,0:T(8,128)(2,1)S(1)} %bitcast.153), kind=kOutput, calls=%fused_computation.3 | convolution fusion | flops 252313600 | bytes 3325952 | tf_op jit(solution)/shard_map/dot_general | solution.py:187
  (75 shorter events, 3.9 us)
Async XLA Ops:
  7.9 0.8 copy-start
  8.7 0.7 copy-start.2
  10.6 25.5 %all-to-all-start = ((bf16[8,88,128]{2,1,0:T(8,128)(2,1)}), bf16[8,88,128]{2,1,0:T(8,128)(2,1)S(1)}, u32[]{:S(2)}, u32[]{:S(2)}) async-start(bf16[8,88,128]{2,1,0:T(8,128)(2,1)} %shard_map.169), calls=%async_computation | async-start | bytes 360448 | tf_op jit(solution)/shard_map/all_to_all | solution.py:122
  20.9 15.2 %collective-permute-start.1 = (bf16[24,5120]{1,0:T(8,128)(2,1)}, bf16[24,5120]{1,0:T(8,128)(2,1)}, u32[]{:S(2)}, u32[]{:S(2)}) collective-permute-start(bf16[24,5120]{1,0:T(8,128)(2,1)} %param.10), channel_id=1, source_target_pairs={{0,1},{1,0},{2,3},{3,2},{4,5},{5,4},{6,7},{7,6},{8,9},{9,8},{10,11... | collective-permute-start | bytes 737288 | tf_op jit(solution)/shard_map/ppermute | solution.py:106
  37.4 7.9 %copy-start.5 = (bf16[1,5120,128]{2,1,0:T(8,128)(2,1)S(1)}, bf16[1,5120,128]{2,1,0:T(8,128)(2,1)}, u32[]{:S(2)}) copy-start(bf16[1,5120,128]{2,1,0:T(8,128)(2,1)} %param.18) | copy-start | bytes 3932164
  37.4 30.6 %all-to-all-start.1 = ((bf16[8,704,128]{2,1,0:T(8,128)(2,1)}), bf16[8,704,128]{2,1,0:T(8,128)(2,1)S(1)}, u32[]{:S(2)}, u32[]{:S(2)}) async-start(bf16[8,704,128]{2,1,0:T(8,128)(2,1)} %broadcast_in_dim.57), calls=%async_computation.1 | async-start | bytes 2883584 | tf_op jit(solution)/shard_map/all_to_all | solution.py:126
  45.3 6.4 %copy-start.6 = (bf16[192,128]{1,0:T(8,128)(2,1)S(1)}, bf16[192,128]{1,0:T(8,128)(2,1)}, u32[]{:S(2)}) copy-start(bf16[192,128]{1,0:T(8,128)(2,1)} %param.11) | copy-start | bytes 147460
  45.3 43.5 %all-gather.2.cloned.1.call-start = ((), (), s32[]{:S(2)}) async-start(), calls=%async_computation.3 | async-start | bytes 2457600 | tf_op jit(solution)/shard_map/all_gather | solution.py:132
  45.4 13.2 %collective-permute-start = (bf16[32,80,128]{2,1,0:T(8,128)(2,1)S(1)}, bf16[32,80,128]{2,1,0:T(8,128)(2,1)}, u32[]{:S(2)}, u32[]{:S(2)}) collective-permute-start(bf16[32,80,128]{2,1,0:T(8,128)(2,1)S(1)} %dynamic-slice_bitcast_fusion), channel_id=1, source_target_pairs={{0,8},{8,0},{1,9},{9,1},{2,10},{10,2},{3,11},{11,3},{4,12},{12,4},... | collective-permute-start | bytes 1966088 | tf_op jit(solution)/shard_map/ppermute | solution.py:140
  51.8 16.3 %collective-permute-start.2 = (bf16[4,24,128]{2,1,0:T(8,128)(2,1)S(1)}, bf16[4,24,128]{2,1,0:T(8,128)(2,1)S(1)}, u32[]{:S(2)}, u32[]{:S(2)}) collective-permute-start(bf16[4,24,128]{2,1,0:T(8,128)(2,1)S(1)} %get-tuple-element.55), channel_id=1, source_target_pairs={{0,1},{1,0},{2,3},{3,2},{4,5},{5,4},{6,7},{7,6},{8,9},{9,8},{10,11... | collective-permute-start | bytes 73736 | tf_op jit(solution)/shard_map/ppermute | solution.py:135
  68.1 15.6 %collective-permute-start.3 = (bf16[8,704,128]{2,1,0:T(8,128)(2,1)S(1)}, bf16[8,704,128]{2,1,0:T(8,128)(2,1)}, u32[]{:S(2)}, u32[]{:S(2)}) collective-permute-start(bf16[8,704,128]{2,1,0:T(8,128)(2,1)S(1)} %all-to-all-done.1), channel_id=1, source_target_pairs={{0,8},{8,0},{1,9},{9,1},{2,10},{10,2},{3,11},{11,3},{4,12},{12,4},... | collective-permute-start | bytes 4325384 | tf_op jit(solution)/shard_map/ppermute | solution.py:145
  72.8 49.1 %all-to-all-start.2 = ((bf16[32,80,128]{2,1,0:T(8,128)(2,1)}), bf16[32,80,128]{2,1,0:T(8,128)(2,1)S(1)}, u32[]{:S(2)}, u32[]{:S(2)}) async-start(bf16[32,80,128]{2,1,0:T(8,128)(2,1)} %fusion.4), calls=%async_computation.2 | async-start | bytes 1310720 | tf_op jit(solution)/shard_map/all_to_all | solution.py:143
  86.7 2.2 %copy-start.7 = (f32[1,96,128]{2,1,0:T(8,128)S(1)}, f32[1,96,128]{2,1,0:T(8,128)}, u32[]{:S(2)}) copy-start(f32[1,96,128]{2,1,0:T(8,128)} %get-tuple-element.52) | copy-start | bytes 147460
  88.8 1.9 %copy-start.3 = (bf16[192,5120]{1,0:T(8,128)(2,1)S(1)}, bf16[192,5120]{1,0:T(8,128)(2,1)}, u32[]{:S(2)}) copy-start(bf16[192,5120]{1,0:T(8,128)(2,1)} %all-gather.2.cloned.1.call-done) | copy-start | bytes 5898244
  101.9 10.2 %copy-start.10 = (pred[8]{0:T(512)(128)(4,1)S(1)}, pred[8]{0:T(512)(128)(4,1)}, u32[]{:S(2)}) copy-start(pred[8]{0:T(512)(128)(4,1)} %iota_compare_fusion.2) | copy-start | bytes 28
  101.9 10.2 %copy-start.11 = (pred[8]{0:T(512)(128)(4,1)S(1)}, pred[8]{0:T(512)(128)(4,1)}, u32[]{:S(2)}) copy-start(pred[8]{0:T(512)(128)(4,1)} %get-tuple-element.71) | copy-start | bytes 28
  102.0 10.2 %copy-start.12 = (pred[8]{0:T(512)(128)(4,1)S(1)}, pred[8]{0:T(512)(128)(4,1)}, u32[]{:S(2)}) copy-start(pred[8]{0:T(512)(128)(4,1)} %get-tuple-element.72) | copy-start | bytes 28
  102.0 16.3 %copy-start.13 = (f32[2,1]{0,1:T(1,128)S(1)}, f32[2,1]{0,1:T(1,128)}, u32[]{:S(2)}) copy-start(f32[2,1]{0,1:T(1,128)} %param.15) | copy-start | bytes 28
  102.0 16.3 %copy-start.14 = (f32[2,1]{0,1:T(1,128)S(1)}, f32[2,1]{0,1:T(1,128)}, u32[]{:S(2)}) copy-start(f32[2,1]{0,1:T(1,128)} %param.16) | copy-start | bytes 28
  102.0 16.3 %copy-start.15 = (f32[2,1]{0,1:T(1,128)S(1)}, f32[2,1]{0,1:T(1,128)}, u32[]{:S(2)}) copy-start(f32[2,1]{0,1:T(1,128)} %param.17) | copy-start | bytes 28
  102.1 20.5 %copy-start.1 = (f32[80,128]{1,0:T(8,128)S(1)}, f32[80,128]{1,0:T(8,128)}, u32[]{:S(2)}) copy-start(f32[80,128]{1,0:T(8,128)} %weight_ref.1) | copy-start | bytes 122884
  102.1 20.5 %copy-start.8 = (f32[80,128]{1,0:T(8,128)S(1)}, f32[80,128]{1,0:T(8,128)}, u32[]{:S(2)}) copy-start(f32[80,128]{1,0:T(8,128)} %param.13) | copy-start | bytes 122884
  102.1 20.5 %copy-start.9 = (f32[80,128]{1,0:T(8,128)S(1)}, f32[80,128]{1,0:T(8,128)}, u32[]{:S(2)}) copy-start(f32[80,128]{1,0:T(8,128)} %param.14) | copy-start | bytes 122884
  102.1 21.1 %copy-start.4 = (bf16[192,5120]{1,0:T(8,128)(2,1)S(1)}, bf16[192,5120]{1,0:T(8,128)(2,1)}, u32[]{:S(2)}) copy-start(bf16[192,5120]{1,0:T(8,128)(2,1)} %all-gather.2.cloned.1.call-done) | copy-start | bytes 5898244
  102.1 16.8 %collective-permute-start.5 = (bf16[24,5120]{1,0:T(8,128)(2,1)S(1)}, bf16[24,5120]{1,0:T(8,128)(2,1)S(1)}, u32[]{:S(2)}, u32[]{:S(2)}) collective-permute-start(bf16[24,5120]{1,0:T(8,128)(2,1)S(1)} %get-tuple-element.45), channel_id=1, source_target_pairs={{0,4},{2,6},{4,0},{6,2},{1,5},{3,7},{5,1},{7,3},{8,12},{10,14},{12... | collective-permute-start | bytes 737288 | tf_op jit(solution)/shard_map/ppermute | solution.py:82
  105.0 14.0 %collective-permute-start.6 = (bf16[24,5120]{1,0:T(8,128)(2,1)S(1)}, bf16[24,5120]{1,0:T(8,128)(2,1)S(1)}, u32[]{:S(2)}, u32[]{:S(2)}) collective-permute-start(bf16[24,5120]{1,0:T(8,128)(2,1)S(1)} %get-tuple-element.47), channel_id=1, source_target_pairs={{0,2},{2,4},{4,6},{6,0},{1,3},{3,5},{5,7},{7,1},{8,10},{10,12},{12... | collective-permute-start | bytes 737288 | tf_op jit(solution)/shard_map/ppermute | solution.py:82
  107.7 11.3 %collective-permute-start.7 = (bf16[24,5120]{1,0:T(8,128)(2,1)S(1)}, bf16[24,5120]{1,0:T(8,128)(2,1)S(1)}, u32[]{:S(2)}, u32[]{:S(2)}) collective-permute-start(bf16[24,5120]{1,0:T(8,128)(2,1)S(1)} %get-tuple-element.46), channel_id=1, source_target_pairs={{0,6},{2,0},{4,2},{6,4},{1,7},{3,1},{5,3},{7,5},{8,14},{10,8},{12,... | collective-permute-start | bytes 737288 | tf_op jit(solution)/shard_map/ppermute | solution.py:82
  112.2 9.7 %collective-permute-start.4 = (bf16[104,128]{1,0:T(8,128)(2,1)S(1)}, bf16[104,128]{1,0:T(8,128)(2,1)S(1)}, u32[]{:S(2)}, u32[]{:S(2)}) collective-permute-start(bf16[104,128]{1,0:T(8,128)(2,1)S(1)} %maximum_select_fusion.2), channel_id=1, source_target_pairs={{0,1},{1,0},{2,3},{3,2},{4,5},{5,4},{6,7},{7,6},{8,9},{9,8},{10,11... | collective-permute-start | bytes 79880 | tf_op jit(solution)/shard_map/ppermute | solution.py:183
Sparse Core Ops, SparseCore 0:
  51.9 36.9 all-gather.1

commit v5 on v4

--- a/solution.py
+++ b/solution.py
@@ -66,7 +66,9 @@
     lane = lax.broadcasted_iota(jnp.int32, (EXT - ROWS, 128), 1)
     row = lax.broadcasted_iota(jnp.int32, (EXT - ROWS, 128), 0)
     at = 2 * place_ref[0]
-    gains = jnp.where(lane == at, gain_ref[0, 0], jnp.where(lane == at + 1, gain_ref[1, 0], 0.0))
+    gain = gain_ref[...]
+    one, two = (jnp.broadcast_to(gain[:, i : i + 1], lane.shape) for i in range(2))
+    gains = jnp.where(lane == at, one, jnp.where(lane == at + 1, two, 0.0))
     prior = jnp.broadcast_to(prior_ref[...], lane.shape)
     hi = prior.astype(bf16).astype(f32)
     mid = (prior - hi).astype(bf16).astype(f32)
@@ -77,9 +79,9 @@
     out_ref[...] = jnp.broadcast_to(block[None], out_ref.shape)
 
 
-def exchange_x(block_for, mine):
+def exchange(axis, size, block_for, mine):
     return [mine] + [
-        lax.ppermute(block_for(d), "x", [(i, (i + d) % NX) for i in range(NX)])
+        lax.ppermute(block_for(d), axis, [(i, (i + d) % size) for i in range(size)])
         for d in (2, 1, 3)
     ]
 
@@ -111,34 +113,34 @@
         out_shape=jax.ShapeDtypeStruct((NZ, EXT, 128), bf16),
         in_specs=[
             pl.BlockSpec(memory_space=pltpu.SMEM),
-            pl.BlockSpec(memory_space=pltpu.SMEM),
+            pl.BlockSpec(memory_space=pltpu.VMEM),
             pl.BlockSpec(memory_space=pltpu.VMEM),
             pl.BlockSpec(memory_space=pltpu.VMEM),
         ],
         out_specs=pl.BlockSpec(memory_space=pltpu.VMEM),
         compiler_params=pltpu.CompilerParams(vmem_limit_bytes=16 * 1024 * 1024),
-    )(dp.reshape(1), gain_master_copy, prior_gain_gradient.reshape(1, 128), weight_master)
+    )(dp.reshape(1), gain_master_copy.T, prior_gain_gradient.reshape(1, 128), weight_master)
     along_z, along_y = [rings(core, True) for core in range(NC)], [rings(core, False) for core in range(NC)]
     first = lax.all_to_all(
         shards, AXES, 0, 0, tiled=True, axis_index_groups=along_z[0] + along_y[1]
     )
-    first, partner = lax.optimization_barrier((first, partner))
+    rows = jnp.concatenate([token_features, partner], axis=0)
+
+    prev = weight_grad_prev.reshape(NZ * NYL, NC, ROWS, 128)
+    other_core = lax.ppermute(pick(prev, 1 - c, 1), "c", SWAP)
+    pair = (pick(prev, c, 1).astype(f32) + other_core.astype(f32)).astype(bf16)
+
+    cot = key_cotangent.reshape(NX, NYH, own, 128)
+    cot_got = lax.ppermute(pick(cot, 1 - yh, 1), "yh", SWAP)
+    cot_two = ordered(pick(cot, yh, 1), cot_got, yh).reshape(NYH, half, 128).astype(f32)
+
+    first, rows, pair, cot_two = lax.optimization_barrier((first, rows, pair, cot_two))
+    rows = lax.all_gather(rows, "x", axis=0, tiled=True)
     gathered = lax.all_to_all(
         jnp.broadcast_to(first.reshape(1, -1, 128), (ring, NZ * EXT, 128)),
         AXES, 0, 0, tiled=True, axis_index_groups=along_y[0] + along_z[1],
     )
 
-    rows = jnp.concatenate([token_features, partner], axis=0)
-    rows = lax.all_gather(rows, "x", axis=0, tiled=True)
-
-    cot = key_cotangent.reshape(NX, NYH, own, 128)
-    cot_got = lax.ppermute(pick(cot, 1 - yh, 1), "yh", SWAP)
-    gathered, cot_got = lax.optimization_barrier((gathered, cot_got))
-    cot_two = ordered(pick(cot, yh, 1), cot_got, yh).reshape(NYH, half, 128).astype(f32)
-
-    prev = weight_grad_prev.reshape(NZ * NYL, NC, ROWS, 128)
-    other_core = lax.ppermute(pick(prev, 1 - c, 1), "c", SWAP)
-    pair = (pick(prev, c, 1).astype(f32) + other_core.astype(f32)).astype(bf16)
     pair, gathered = lax.optimization_barrier((pair, gathered))
     arrived = lax.all_to_all(pair, ("z", "yl"), 0, 0, tiled=True)
 
@@ -173,7 +175,7 @@
         for h in range(NYH)
     )
     terms = terms.astype(bf16).reshape(NX, own, width)
-    received = exchange_x(lambda d: pick(terms, lax.rem(x + d, NX), 0), pick(terms, x, 0))
+    received = exchange("x", NX, lambda d: pick(terms, lax.rem(x + d, NX), 0), pick(terms, x, 0))
     input_grad = sum(block.astype(f32) for block in received).astype(bf16)
 
     both_grads = jnp.stack(grads)

time: 133 us -> 130 us (0.977)
  starting transfers between devices: 66.1 us -> 51.8 us
  waiting for transfers between devices: 19.9 us -> 32 us
  other arithmetic: 10.7 us -> 9.11 us
    all_to_all x1, waiting for transfers between devices: 0.01 us -> 20.9 us  [local(): lax.all_to_all(jnp.broadcast_to(first.reshape(1, -1, 128), (ring, NZ * EX...]
    ppermute x1, waiting for transfers between devices: 8.39 us -> 0.01 us  [local(): partner = lax.ppermute(token_features, 'yh', SWAP)]
    ppermute x1, waiting for transfers between devices: 7.35 us -> 0.01 us  [local(): cot_got = lax.ppermute(pick(cot, 1 - yh, 1), 'yh', SWAP)]
    all_to_all x1, waiting for transfers between devices: 0.01 us -> 6.74 us  [local(): lax.all_to_all(shards, AXES, 0, 0, tiled=True, axis_index_groups=along_z[...]
    all_to_all x1, starting transfers between devices: 10.2 us -> 5.06 us  [local(): arrived = lax.all_to_all(pair, ('z', 'yl'), 0, 0, tiled=True)]
    ppermute x1, starting transfers between devices: 6.78 us -> 2.9 us  [local(): cot_got = lax.ppermute(pick(cot, 1 - yh, 1), 'yh', SWAP)]
    ppermute x1, starting transfers between devices: 4.44 us -> 1.92 us  [local(): other_core = lax.ppermute(pick(prev, 1 - c, 1), 'c', SWAP)]
    unnamed x33 -> x26, local copies, waits for them, and re-layouts: 2.25 us -> 0.07 us
  transfers between devices with their start and end apart: 12 -> 12, of which waited for: 4 -> 4; matrix products, arithmetic and copies ran while one was open for 11% -> 12% of each run, Pallas kernels for 0% -> 1%
where the time goes in v5:
time: 130 us; the launch traced here: 129 us
  starting transfers between devices  51.8 us (40%)
  waiting for transfers between devices  32 us (25%)
  between operations  14.5 us (11%)
  blocking collectives  9.81 us (8%)
  other arithmetic  9.11 us (7%)
  matrix products  6.39 us (5%)
  local copies, waits for them, and re-layouts  4.78 us (4%)
    all_to_all x1, waiting for transfers between devices, local(): lax.all_to_all(jnp.broadcast_to(first.reshape(1, -1, 128), (ring, NZ * EX...  20.9 us
    all_to_all x1, starting transfers between devices, local(): lax.all_to_all(shards, AXES, 0, 0, tiled=True, axis_index_groups=along_z[...  10.3 us
    ppermute x3, starting transfers between devices, exchange(): lax.ppermute(block_for(d), axis, [(i, (i + d) % size) for i in range(size)])  9.95 us
    psum x1, blocking collectives, local(): squares, cross = lax.psum(sums, 'x')  9.81 us
    all_to_all x1, starting transfers between devices, local(): lax.all_to_all(jnp.broadcast_to(first.reshape(1, -1, 128), (ring, NZ * EX...  7.55 us
    ppermute x1, starting transfers between devices, local(): partner = lax.ppermute(token_features, 'yh', SWAP)  6.97 us
    all_to_all x1, waiting for transfers between devices, local(): lax.all_to_all(shards, AXES, 0, 0, tiled=True, axis_index_groups=along_z[...  6.74 us
    ppermute x1, starting transfers between devices, local(): got = lax.ppermute(jnp.where(yh == 0, give[1], give[0]), 'yh', SWAP)  5.25 us
  transfers between devices with their start and end apart: 12, of which 4 were waited for; matrix products, arithmetic and copies ran while one was open for 12% of the time, Pallas kernels for 1%

profile of v5, /device:TPU:8, one launch (start us, length us, event | category | flops | bytes accessed | tf_op | source)
XLA Modules:
  0.0 129.2 jit_solution(11621423844502240265)
XLA Ops:
  7.2 7.0 %collective-permute-start = (bf16[24,5120]{1,0:T(8,128)(2,1)}, bf16[24,5120]{1,0:T(8,128)(2,1)}, u32[]{:S(2)}, u32[]{:S(2)}) collective-permute-start(bf16[24,5120]{1,0:T(8,128)(2,1)} %param.10), channel_id=1, source_target_pairs={{0,1},{1,0},{2,3},{3,2},{4,5},{5,4},{6,7},{7,6},{8,9},{9,8},{10,11... | collective-permute-start | bytes 737288 | tf_op jit(solution)/shard_map/ppermute | solution.py:108
  14.2 0.8 constant_dynamic-slice_fusion.2
  15.0 2.9 %collective-permute-start.2 = (bf16[4,24,128]{2,1,0:T(8,128)(2,1)S(1)}, bf16[4,24,128]{2,1,0:T(8,128)(2,1)S(1)}, u32[]{:S(2)}, u32[]{:S(2)}) collective-permute-start(bf16[4,24,128]{2,1,0:T(8,128)(2,1)S(1)} %get-tuple-element.55), channel_id=1, source_target_pairs={{0,1},{1,0},{2,3},{3,2},{4,5},{5,4},{6,7},{7,6},{8,9},{9,8},{10,11... | collective-permute-start | bytes 73736 | tf_op jit(solution)/shard_map/ppermute | solution.py:134
  17.9 1.2 dynamic-slice_bitcast_fusion
  19.1 1.9 %collective-permute-start.1 = (bf16[32,80,128]{2,1,0:T(8,128)(2,1)S(1)}, bf16[32,80,128]{2,1,0:T(8,128)(2,1)S(1)}, u32[]{:S(2)}, u32[]{:S(2)}) collective-permute-start(bf16[32,80,128]{2,1,0:T(8,128)(2,1)S(1)} %dynamic-slice_bitcast_fusion), channel_id=1, source_target_pairs={{0,8},{8,0},{1,9},{9,1},{2,10},{10,2},{3,11},{11,3},{4,12},{12,4},... | collective-permute-start | bytes 1966088 | tf_op jit(solution)/shard_map/ppermute | solution.py:130
  21.1 0.8 shard_map.169
  21.9 10.3 %all-to-all-start = ((bf16[8,88,128]{2,1,0:T(8,128)(2,1)}), bf16[8,88,128]{2,1,0:T(8,128)(2,1)S(1)}, u32[]{:S(2)}, u32[]{:S(2)}) async-start(bf16[8,88,128]{2,1,0:T(8,128)(2,1)} %shard_map.169), calls=%async_computation | async-start | bytes 360448 | tf_op jit(solution)/shard_map/all_to_all | solution.py:124
  32.2 1.8 %pad_maximum_fusion = bf16[48,5120]{1,0:T(8,128)(2,1)} fusion(bf16[24,5120]{1,0:T(8,128)(2,1)} %collective-permute-done, bf16[24,5120]{1,0:T(8,128)(2,1)S(1)} %copy-done.6), kind=kLoop, calls=%fused_computation.17 | loop fusion | flops 983040 | bytes 983040 | tf_op jit(solution)/shard_map/concatenate | solution.py:127
  34.0 1.0 fusion.4
  35.0 6.7 %all-to-all-done = bf16[8,88,128]{2,1,0:T(8,128)(2,1)S(1)} async-done(((bf16[8,88,128]{2,1,0:T(8,128)(2,1)}), bf16[8,88,128]{2,1,0:T(8,128)(2,1)S(1)}, u32[]{:S(2)}, u32[]{:S(2)}) %all-to-all-start) | async-done | bytes 180256 | tf_op jit(solution)/shard_map/all_to_all | solution.py:124
  41.8 1.3 %broadcast_in_dim.57 = bf16[8,704,128]{2,1,0:T(8,128)(2,1)} broadcast(bf16[704,128]{1,0:T(8,128)(2,1)S(1)} %bitcast.152), dimensions={1,2} | broadcast | bytes 1622016 | tf_op jit(solution)/shard_map/broadcast_in_dim | solution.py:140
  43.1 7.5 %all-to-all-start.1 = ((bf16[8,704,128]{2,1,0:T(8,128)(2,1)}), bf16[8,704,128]{2,1,0:T(8,128)(2,1)S(1)}, u32[]{:S(2)}, u32[]{:S(2)}) async-start(bf16[8,704,128]{2,1,0:T(8,128)(2,1)} %broadcast_in_dim.57), calls=%async_computation.1 | async-start | bytes 2883584 | tf_op jit(solution)/shard_map/all_to_all | solution.py:139
  50.6 0.7 all-gather.2.cloned.1.call-update
  51.3 20.9 %all-to-all-done.1 = bf16[8,704,128]{2,1,0:T(8,128)(2,1)S(1)} async-done(((bf16[8,704,128]{2,1,0:T(8,128)(2,1)}), bf16[8,704,128]{2,1,0:T(8,128)(2,1)S(1)}, u32[]{:S(2)}, u32[]{:S(2)}) %all-to-all-start.1) | async-done | bytes 1441824 | tf_op jit(solution)/shard_map/all_to_all | solution.py:139
  72.3 1.9 %collective-permute-start.3 = (bf16[8,704,128]{2,1,0:T(8,128)(2,1)S(1)}, bf16[8,704,128]{2,1,0:T(8,128)(2,1)}, u32[]{:S(2)}, u32[]{:S(2)}) collective-permute-start(bf16[8,704,128]{2,1,0:T(8,128)(2,1)S(1)} %all-to-all-done.1), channel_id=1, source_target_pairs={{0,8},{8,0},{1,9},{9,1},{2,10},{10,2},{3,11},{11,3},{4,12},{12,4},... | collective-permute-start | bytes 4325384 | tf_op jit(solution)/shard_map/ppermute | solution.py:147
  74.8 0.6 fusion.32
  75.4 5.1 %all-to-all-start.2 = ((bf16[32,80,128]{2,1,0:T(8,128)(2,1)}), bf16[32,80,128]{2,1,0:T(8,128)(2,1)S(1)}, u32[]{:S(2)}, u32[]{:S(2)}) async-start(bf16[32,80,128]{2,1,0:T(8,128)(2,1)} %fusion.4), calls=%async_computation.2 | async-start | bytes 1310720 | tf_op jit(solution)/shard_map/all_to_all | solution.py:145
  80.5 2.3 %maximum_select_fusion = bf16[2,8,704,128]{3,2,1,0:T(8,128)(2,1)S(1)} fusion(bf16[1,8,704,128]{3,2,1,0:T(8,128)(2,1)} %bitcast.13, bf16[1,8,704,128]{3,2,1,0:T(8,128)(2,1)S(1)} %bitcast.140, pred[]{:T(512)S(6)} %eq.29), kind=kLoop, calls=%fused_computation.8 | loop fusion | flops 4325376 | bytes 5767169 | tf_op jit(solution)/shard_map/jit(_where)/select_n | solution.py:40
  83.7 0.7 all-gather.2.cloned.1.call-done
  84.4 1.9 %multiply_reduce_fusion.2 = (f32[4,24]{1,0:T(4,128)S(1)}, f32[4,24]{1,0:T(4,128)S(1)}, f32[4,1,24,128]{3,2,1,0:T(8,128)S(1)}) fusion(f32[4,1,24,128]{3,2,1,0:T(8,128)S(1)} %bitcast.161, f32[128]{0:T(128)S(1)} %get-tuple-element.56, bf16[4,2,24,5120]{3,2,1,0:T(8,128)(2,1)} %bitcast.148, bf16[5120,128,1,1]{1,0,3,2:T(8,128)(2,1)S(1)} %bitcast.144), kind=kOutput, calls=%fused_computation.50 | convolution fusion | flops 125890368 | bytes 3376384 | tf_op jit(solution)/shard_map/slice | solution.py:158
  86.4 1.4 %multiply_reduce_fusion.3 = (f32[4,24]{1,0:T(4,128)S(1)}, f32[4,24]{1,0:T(4,128)S(1)}, f32[4,1,24,128]{3,2,1,0:T(8,128)S(1)}) fusion(f32[4,1,24,128]{3,2,1,0:T(8,128)} %bitcast.160, f32[128]{0:T(128)S(1)} %get-tuple-element.57, bf16[4,2,24,5120]{3,2,1,0:T(8,128)(2,1)S(1)} %bitcast.149, bf16[5120,128,1,1]{1,0,3,2:T(8,128)(2,1)S(1)} %bitcast.142), kind=kOutput, calls=%fused_computation.51 | convolution fusion | flops 125890368 | bytes 3376384 | tf_op jit(solution)/shard_map/slice | solution.py:158
  87.9 9.8 %psum.7 = f32[2,96]{1,0:T(2,128)S(1)} all-reduce(f32[2,96]{1,0:T(2,128)S(1)} %pad_maximum_fusion.3), channel_id=1, replica_groups=mesh['z'=8,'yl'=4,'c'=2,'x'=4,'yh'=2] {'x'}, use_global_device_ids=true, to_apply=%region_5.6 | all-reduce | flops 192 | bytes 1536 | tf_op jit(solution)/shard_map/psum | solution.py:166
  98.5 0.6 fusion
  99.3 2.9 %collective-permute-start.5 = (bf16[24,5120]{1,0:T(8,128)(2,1)S(1)}, bf16[24,5120]{1,0:T(8,128)(2,1)S(1)}, u32[]{:S(2)}, u32[]{:S(2)}) collective-permute-start(bf16[24,5120]{1,0:T(8,128)(2,1)S(1)} %get-tuple-element.45), channel_id=1, source_target_pairs={{0,4},{2,6},{4,0},{6,2},{1,5},{3,7},{5,1},{7,3},{8,12},{10,14},{12... | collective-permute-start | bytes 737288 | tf_op jit(solution)/shard_map/ppermute | solution.py:84
  102.2 1.9 %collective-permute-start.6 = (bf16[24,5120]{1,0:T(8,128)(2,1)S(1)}, bf16[24,5120]{1,0:T(8,128)(2,1)S(1)}, u32[]{:S(2)}, u32[]{:S(2)}) collective-permute-start(bf16[24,5120]{1,0:T(8,128)(2,1)S(1)} %get-tuple-element.47), channel_id=1, source_target_pairs={{0,2},{2,4},{4,6},{6,0},{1,3},{3,5},{5,7},{7,1},{8,10},{10,12},{12... | collective-permute-start | bytes 737288 | tf_op jit(solution)/shard_map/ppermute | solution.py:84
  104.1 5.1 %collective-permute-start.7 = (bf16[24,5120]{1,0:T(8,128)(2,1)S(1)}, bf16[24,5120]{1,0:T(8,128)(2,1)S(1)}, u32[]{:S(2)}, u32[]{:S(2)}) collective-permute-start(bf16[24,5120]{1,0:T(8,128)(2,1)S(1)} %get-tuple-element.46), channel_id=1, source_target_pairs={{0,6},{2,0},{4,2},{6,4},{1,7},{3,1},{5,3},{7,5},{8,14},{10,8},{12,... | collective-permute-start | bytes 737288 | tf_op jit(solution)/shard_map/ppermute | solution.py:84
  109.4 5.2 %collective-permute-start.4 = (bf16[104,128]{1,0:T(8,128)(2,1)S(1)}, bf16[104,128]{1,0:T(8,128)(2,1)S(1)}, u32[]{:S(2)}, u32[]{:S(2)}) collective-permute-start(bf16[104,128]{1,0:T(8,128)(2,1)S(1)} %maximum_select_fusion.2), channel_id=1, source_target_pairs={{0,1},{1,0},{2,3},{3,2},{4,5},{5,4},{6,7},{7,6},{8,9},{9,8},{10,11... | collective-permute-start | bytes 79880 | tf_op jit(solution)/shard_map/ppermute | solution.py:185
  114.7 0.6 multiply_subtract_fusion.1
  115.3 0.8 fusion.7
  116.2 2.9 %collective-permute-done.4 = bf16[104,128]{1,0:T(8,128)(2,1)S(1)} collective-permute-done((bf16[104,128]{1,0:T(8,128)(2,1)S(1)}, bf16[104,128]{1,0:T(8,128)(2,1)S(1)}, u32[]{:S(2)}, u32[]{:S(2)}) %collective-permute-start.4) | collective-permute-done | bytes 26656 | tf_op jit(solution)/shard_map/ppermute | solution.py:185
  119.7 0.7 multiply_subtract_fusion
  120.4 2.0 %fusion.1 = bf16[1,5120,128]{2,1,0:T(8,128)(2,1)} fusion(bf16[192,5120]{1,0:T(8,128)(2,1)S(1)} %copy-done.4, bf16[192,128]{1,0:T(8,128)(2,1)S(1)} %bitcast.155), kind=kOutput, calls=%fused_computation.3 | convolution fusion | flops 252313600 | bytes 3325952 | tf_op jit(solution)/shard_map/dot_general | solution.py:189
  (68 shorter events, 3.3 us)
Async XLA Ops:
  7.2 25.0 %copy-start.6 = (bf16[24,5120]{1,0:T(8,128)(2,1)S(1)}, bf16[24,5120]{1,0:T(8,128)(2,1)}, u32[]{:S(2)}) copy-start(bf16[24,5120]{1,0:T(8,128)(2,1)} %param.10) | copy-start | bytes 737284
  7.2 13.9 %copy-start.1 = (f32[2,1]{0,1:T(1,128)S(1)}, f32[2,1]{0,1:T(1,128)}, u32[]{:S(2)}) copy-start(f32[2,1]{0,1:T(1,128)} %param.15) | copy-start | bytes 28
  7.2 13.9 %copy-start.2 = (f32[1,128,1]{1,2,0:T(1,128)S(1)}, f32[1,128,1]{1,2,0:T(1,128)}, u32[]{:S(2)}) copy-start(f32[1,128,1]{1,2,0:T(1,128)} %param.19) | copy-start | bytes 1540
  7.2 13.9 %copy-start = (f32[80,128]{1,0:T(8,128)S(1)}, f32[80,128]{1,0:T(8,128)}, u32[]{:S(2)}) copy-start(f32[80,128]{1,0:T(8,128)} %weight_ref.1) | copy-start | bytes 122884
  7.2 25.0 %collective-permute-start = (bf16[24,5120]{1,0:T(8,128)(2,1)}, bf16[24,5120]{1,0:T(8,128)(2,1)}, u32[]{:S(2)}, u32[]{:S(2)}) collective-permute-start(bf16[24,5120]{1,0:T(8,128)(2,1)} %param.10), channel_id=1, source_target_pairs={{0,1},{1,0},{2,3},{3,2},{4,5},{5,4},{6,7},{7,6},{8,9},{9,8},{10,11... | collective-permute-start | bytes 737288 | tf_op jit(solution)/shard_map/ppermute | solution.py:108
  15.0 17.2 %collective-permute-start.2 = (bf16[4,24,128]{2,1,0:T(8,128)(2,1)S(1)}, bf16[4,24,128]{2,1,0:T(8,128)(2,1)S(1)}, u32[]{:S(2)}, u32[]{:S(2)}) collective-permute-start(bf16[4,24,128]{2,1,0:T(8,128)(2,1)S(1)} %get-tuple-element.55), channel_id=1, source_target_pairs={{0,1},{1,0},{2,3},{3,2},{4,5},{5,4},{6,7},{7,6},{8,9},{9,8},{10,11... | collective-permute-start | bytes 73736 | tf_op jit(solution)/shard_map/ppermute | solution.py:134
  17.9 16.1 %copy-start.5 = (bf16[1,5120,128]{2,1,0:T(8,128)(2,1)S(1)}, bf16[1,5120,128]{2,1,0:T(8,128)(2,1)}, u32[]{:S(2)}) copy-start(bf16[1,5120,128]{2,1,0:T(8,128)(2,1)} %param.18) | copy-start | bytes 3932164
  19.1 14.9 %collective-permute-start.1 = (bf16[32,80,128]{2,1,0:T(8,128)(2,1)S(1)}, bf16[32,80,128]{2,1,0:T(8,128)(2,1)S(1)}, u32[]{:S(2)}, u32[]{:S(2)}) collective-permute-start(bf16[32,80,128]{2,1,0:T(8,128)(2,1)S(1)} %dynamic-slice_bitcast_fusion), channel_id=1, source_target_pairs={{0,8},{8,0},{1,9},{9,1},{2,10},{10,2},{3,11},{11,3},{4,12},{12,4},... | collective-permute-start | bytes 1966088 | tf_op jit(solution)/shard_map/ppermute | solution.py:130
  21.9 19.9 %all-to-all-start = ((bf16[8,88,128]{2,1,0:T(8,128)(2,1)}), bf16[8,88,128]{2,1,0:T(8,128)(2,1)S(1)}, u32[]{:S(2)}, u32[]{:S(2)}) async-start(bf16[8,88,128]{2,1,0:T(8,128)(2,1)} %shard_map.169), calls=%async_computation | async-start | bytes 360448 | tf_op jit(solution)/shard_map/all_to_all | solution.py:124
  43.1 29.2 %all-to-all-start.1 = ((bf16[8,704,128]{2,1,0:T(8,128)(2,1)}), bf16[8,704,128]{2,1,0:T(8,128)(2,1)S(1)}, u32[]{:S(2)}, u32[]{:S(2)}) async-start(bf16[8,704,128]{2,1,0:T(8,128)(2,1)} %broadcast_in_dim.57), calls=%async_computation.1 | async-start | bytes 2883584 | tf_op jit(solution)/shard_map/all_to_all | solution.py:139
  50.6 33.8 %all-gather.2.cloned.1.call-start = ((), (), s32[]{:S(2)}) async-start(), calls=%async_computation.3 | async-start | bytes 2457600 | tf_op jit(solution)/shard_map/all_gather | solution.py:138
  72.3 8.2 %collective-permute-start.3 = (bf16[8,704,128]{2,1,0:T(8,128)(2,1)S(1)}, bf16[8,704,128]{2,1,0:T(8,128)(2,1)}, u32[]{:S(2)}, u32[]{:S(2)}) collective-permute-start(bf16[8,704,128]{2,1,0:T(8,128)(2,1)S(1)} %all-to-all-done.1), channel_id=1, source_target_pairs={{0,8},{8,0},{1,9},{9,1},{2,10},{10,2},{3,11},{11,3},{4,12},{12,4},... | collective-permute-start | bytes 4325384 | tf_op jit(solution)/shard_map/ppermute | solution.py:147
  75.4 43.6 %all-to-all-start.2 = ((bf16[32,80,128]{2,1,0:T(8,128)(2,1)}), bf16[32,80,128]{2,1,0:T(8,128)(2,1)S(1)}, u32[]{:S(2)}, u32[]{:S(2)}) async-start(bf16[32,80,128]{2,1,0:T(8,128)(2,1)} %fusion.4), calls=%async_computation.2 | async-start | bytes 1310720 | tf_op jit(solution)/shard_map/all_to_all | solution.py:145
  84.4 1.9 %copy-start.3 = (bf16[192,5120]{1,0:T(8,128)(2,1)S(1)}, bf16[192,5120]{1,0:T(8,128)(2,1)}, u32[]{:S(2)}) copy-start(bf16[192,5120]{1,0:T(8,128)(2,1)} %all-gather.2.cloned.1.call-done) | copy-start | bytes 5898244
  99.1 10.1 %copy-start.9 = (pred[8]{0:T(512)(128)(4,1)S(1)}, pred[8]{0:T(512)(128)(4,1)}, u32[]{:S(2)}) copy-start(pred[8]{0:T(512)(128)(4,1)} %get-tuple-element.71) | copy-start | bytes 28
  99.1 10.1 %copy-start.10 = (pred[8]{0:T(512)(128)(4,1)S(1)}, pred[8]{0:T(512)(128)(4,1)}, u32[]{:S(2)}) copy-start(pred[8]{0:T(512)(128)(4,1)} %get-tuple-element.72) | copy-start | bytes 28
  99.1 15.5 %copy-start.11 = (f32[2,1]{0,1:T(1,128)S(1)}, f32[2,1]{0,1:T(1,128)}, u32[]{:S(2)}) copy-start(f32[2,1]{0,1:T(1,128)} %param.16) | copy-start | bytes 28
  99.1 15.5 %copy-start.12 = (f32[2,1]{0,1:T(1,128)S(1)}, f32[2,1]{0,1:T(1,128)}, u32[]{:S(2)}) copy-start(f32[2,1]{0,1:T(1,128)} %param.17) | copy-start | bytes 28
  99.2 20.4 %copy-start.7 = (f32[80,128]{1,0:T(8,128)S(1)}, f32[80,128]{1,0:T(8,128)}, u32[]{:S(2)}) copy-start(f32[80,128]{1,0:T(8,128)} %param.13) | copy-start | bytes 122884
  99.2 20.4 %copy-start.8 = (f32[80,128]{1,0:T(8,128)S(1)}, f32[80,128]{1,0:T(8,128)}, u32[]{:S(2)}) copy-start(f32[80,128]{1,0:T(8,128)} %param.14) | copy-start | bytes 122884
  99.2 21.1 %copy-start.4 = (bf16[192,5120]{1,0:T(8,128)(2,1)S(1)}, bf16[192,5120]{1,0:T(8,128)(2,1)}, u32[]{:S(2)}) copy-start(bf16[192,5120]{1,0:T(8,128)(2,1)} %all-gather.2.cloned.1.call-done) | copy-start | bytes 5898244
  99.3 16.0 %collective-permute-start.5 = (bf16[24,5120]{1,0:T(8,128)(2,1)S(1)}, bf16[24,5120]{1,0:T(8,128)(2,1)S(1)}, u32[]{:S(2)}, u32[]{:S(2)}) collective-permute-start(bf16[24,5120]{1,0:T(8,128)(2,1)S(1)} %get-tuple-element.45), channel_id=1, source_target_pairs={{0,4},{2,6},{4,0},{6,2},{1,5},{3,7},{5,1},{7,3},{8,12},{10,14},{12... | collective-permute-start | bytes 737288 | tf_op jit(solution)/shard_map/ppermute | solution.py:84
  102.2 13.2 %collective-permute-start.6 = (bf16[24,5120]{1,0:T(8,128)(2,1)S(1)}, bf16[24,5120]{1,0:T(8,128)(2,1)S(1)}, u32[]{:S(2)}, u32[]{:S(2)}) collective-permute-start(bf16[24,5120]{1,0:T(8,128)(2,1)S(1)} %get-tuple-element.47), channel_id=1, source_target_pairs={{0,2},{2,4},{4,6},{6,0},{1,3},{3,5},{5,7},{7,1},{8,10},{10,12},{12... | collective-permute-start | bytes 737288 | tf_op jit(solution)/shard_map/ppermute | solution.py:84
  104.1 11.2 %collective-permute-start.7 = (bf16[24,5120]{1,0:T(8,128)(2,1)S(1)}, bf16[24,5120]{1,0:T(8,128)(2,1)S(1)}, u32[]{:S(2)}, u32[]{:S(2)}) collective-permute-start(bf16[24,5120]{1,0:T(8,128)(2,1)S(1)} %get-tuple-element.46), channel_id=1, source_target_pairs={{0,6},{2,0},{4,2},{6,4},{1,7},{3,1},{5,3},{7,5},{8,14},{10,8},{12,... | collective-permute-start | bytes 737288 | tf_op jit(solution)/shard_map/ppermute | solution.py:84
  109.4 9.7 %collective-permute-start.4 = (bf16[104,128]{1,0:T(8,128)(2,1)S(1)}, bf16[104,128]{1,0:T(8,128)(2,1)S(1)}, u32[]{:S(2)}, u32[]{:S(2)}) collective-permute-start(bf16[104,128]{1,0:T(8,128)(2,1)S(1)} %maximum_select_fusion.2), channel_id=1, source_target_pairs={{0,1},{1,0},{2,3},{3,2},{4,5},{5,4},{6,7},{7,6},{8,9},{9,8},{10,11... | collective-permute-start | bytes 79880 | tf_op jit(solution)/shard_map/ppermute | solution.py:185
Sparse Core Ops, SparseCore 0:
  53.6 30.8 all-gather.1

commit v6 on v5

--- a/solution.py
+++ b/solution.py
@@ -82,7 +82,7 @@
 def exchange(axis, size, block_for, mine):
     return [mine] + [
         lax.ppermute(block_for(d), axis, [(i, (i + d) % size) for i in range(size)])
-        for d in (2, 1, 3)
+        for d in (1, 3, 2)
     ]
 
 
@@ -183,7 +183,10 @@
         [both_grads[1], split3(gain_terms[1:2], 8)]
     )
     got = lax.ppermute(jnp.where(yh == 0, give[1], give[0]), "yh", SWAP)
-    got, input_grad = lax.optimization_barrier((got, input_grad))
+    arrived, input_grad = lax.optimization_barrier((arrived, input_grad))
+    summed_w = jnp.sum(arrived.astype(f32), axis=0)
+    new_weight = adamw(weight_master, weight_first, weight_second, summed_w, weight_decay)
+    got, input_grad, new_weight = lax.optimization_barrier((got, input_grad, new_weight))
     kept = pick(both_grads, yh, 0).reshape(NX, 1, own, 128)
     group_grad = jnp.concatenate([kept, got[:half].reshape(NX, 1, own, 128)], axis=1)
     weight_grad = lax.dot_general(
@@ -192,10 +195,7 @@
     gain_partner = jnp.sum(got[half:].astype(f32), axis=0)
     gain_grad = (pick(gain_terms, yh, 0) + gain_partner).reshape(1, 128, 1)
 
-    arrived, input_grad = lax.optimization_barrier((arrived, input_grad))
-    summed_w = jnp.sum(arrived.astype(f32), axis=0)
     summed_g = lax.dynamic_slice(summed_g, (2 * dp,), (2,)).reshape(2, 1)
-    new_weight = adamw(weight_master, weight_first, weight_second, summed_w, weight_decay)
     new_gain = adamw(gain_master_copy, gain_first_moment, gain_second_moment, summed_g, 0.0)
     return (input_grad, weight_grad, gain_grad, *new_weight, *new_gain)
 

time: 130 us -> 129 us (level)
  the two profiles are of different devices: /device:TPU:8 before, /device:TPU:12 now
where the time goes in v6:
time: 129 us; the launch traced here: 128 us
  starting transfers between devices  53.6 us (42%)
  waiting for transfers between devices  30.5 us (24%)
  between operations  14.5 us (11%)
  other arithmetic  9.12 us (7%)
  blocking collectives  8.32 us (6%)
  matrix products  6.4 us (5%)
  local copies, waits for them, and re-layouts  4.78 us (4%)
    all_to_all x1, waiting for transfers between devices, local(): lax.all_to_all(jnp.broadcast_to(first.reshape(1, -1, 128), (ring, NZ * EX...  20.9 us
    ppermute x3, starting transfers between devices, exchange(): lax.ppermute(block_for(d), axis, [(i, (i + d) % size) for i in range(size)])  11.8 us
    all_to_all x1, starting transfers between devices, local(): lax.all_to_all(shards, AXES, 0, 0, tiled=True, axis_index_groups=along_z[...  10.3 us
    psum x1, blocking collectives, local(): squares, cross = lax.psum(sums, 'x')  8.32 us
    all_to_all x1, starting transfers between devices, local(): lax.all_to_all(jnp.broadcast_to(first.reshape(1, -1, 128), (ring, NZ * EX...  7.55 us
    ppermute x1, starting transfers between devices, local(): partner = lax.ppermute(token_features, 'yh', SWAP)  6.97 us
    all_to_all x1, waiting for transfers between devices, local(): lax.all_to_all(shards, AXES, 0, 0, tiled=True, axis_index_groups=along_z[...  6.74 us
    ppermute x1, starting transfers between devices, local(): got = lax.ppermute(jnp.where(yh == 0, give[1], give[0]), 'yh', SWAP)  5.25 us
  transfers between devices with their start and end apart: 12, of which 3 were waited for; matrix products, arithmetic and copies ran while one was open for 13% of the time, Pallas kernels for 1%

profile of v6, /device:TPU:12, one launch (start us, length us, event | category | flops | bytes accessed | tf_op | source)
XLA Modules:
  0.0 128.0 jit_solution(2717397821522706230)
XLA Ops:
  7.2 7.0 %collective-permute-start = (bf16[24,5120]{1,0:T(8,128)(2,1)}, bf16[24,5120]{1,0:T(8,128)(2,1)}, u32[]{:S(2)}, u32[]{:S(2)}) collective-permute-start(bf16[24,5120]{1,0:T(8,128)(2,1)} %param.10), channel_id=1, source_target_pairs={{0,1},{1,0},{2,3},{3,2},{4,5},{5,4},{6,7},{7,6},{8,9},{9,8},{10,11... | collective-permute-start | bytes 737288 | tf_op jit(solution)/shard_map/ppermute | solution.py:108
  14.2 0.8 constant_dynamic-slice_fusion.2
  15.0 2.9 %collective-permute-start.2 = (bf16[4,24,128]{2,1,0:T(8,128)(2,1)S(1)}, bf16[4,24,128]{2,1,0:T(8,128)(2,1)S(1)}, u32[]{:S(2)}, u32[]{:S(2)}) collective-permute-start(bf16[4,24,128]{2,1,0:T(8,128)(2,1)S(1)} %get-tuple-element.61), channel_id=1, source_target_pairs={{0,1},{1,0},{2,3},{3,2},{4,5},{5,4},{6,7},{7,6},{8,9},{9,8},{10,11... | collective-permute-start | bytes 73736 | tf_op jit(solution)/shard_map/ppermute | solution.py:134
  17.9 1.2 dynamic-slice_bitcast_fusion
  19.1 1.9 %collective-permute-start.1 = (bf16[32,80,128]{2,1,0:T(8,128)(2,1)S(1)}, bf16[32,80,128]{2,1,0:T(8,128)(2,1)S(1)}, u32[]{:S(2)}, u32[]{:S(2)}) collective-permute-start(bf16[32,80,128]{2,1,0:T(8,128)(2,1)S(1)} %dynamic-slice_bitcast_fusion), channel_id=1, source_target_pairs={{0,8},{8,0},{1,9},{9,1},{2,10},{10,2},{3,11},{11,3},{4,12},{12,4},... | collective-permute-start | bytes 1966088 | tf_op jit(solution)/shard_map/ppermute | solution.py:130
  21.1 0.8 shard_map.169
  21.9 10.3 %all-to-all-start = ((bf16[8,88,128]{2,1,0:T(8,128)(2,1)}), bf16[8,88,128]{2,1,0:T(8,128)(2,1)S(1)}, u32[]{:S(2)}, u32[]{:S(2)}) async-start(bf16[8,88,128]{2,1,0:T(8,128)(2,1)} %shard_map.169), calls=%async_computation | async-start | bytes 360448 | tf_op jit(solution)/shard_map/all_to_all | solution.py:124
  32.2 1.8 %pad_maximum_fusion = bf16[48,5120]{1,0:T(8,128)(2,1)} fusion(bf16[24,5120]{1,0:T(8,128)(2,1)} %collective-permute-done, bf16[24,5120]{1,0:T(8,128)(2,1)S(1)} %copy-done.6), kind=kLoop, calls=%fused_computation.17 | loop fusion | flops 983040 | bytes 983040 | tf_op jit(solution)/shard_map/concatenate | solution.py:127
  34.0 1.0 fusion.4
  35.0 6.7 %all-to-all-done = bf16[8,88,128]{2,1,0:T(8,128)(2,1)S(1)} async-done(((bf16[8,88,128]{2,1,0:T(8,128)(2,1)}), bf16[8,88,128]{2,1,0:T(8,128)(2,1)S(1)}, u32[]{:S(2)}, u32[]{:S(2)}) %all-to-all-start) | async-done | bytes 180256 | tf_op jit(solution)/shard_map/all_to_all | solution.py:124
  41.8 1.3 %broadcast_in_dim.57 = bf16[8,704,128]{2,1,0:T(8,128)(2,1)} broadcast(bf16[704,128]{1,0:T(8,128)(2,1)S(1)} %bitcast.152), dimensions={1,2} | broadcast | bytes 1622016 | tf_op jit(solution)/shard_map/broadcast_in_dim | solution.py:140
  43.1 7.5 %all-to-all-start.1 = ((bf16[8,704,128]{2,1,0:T(8,128)(2,1)}), bf16[8,704,128]{2,1,0:T(8,128)(2,1)S(1)}, u32[]{:S(2)}, u32[]{:S(2)}) async-start(bf16[8,704,128]{2,1,0:T(8,128)(2,1)} %broadcast_in_dim.57), calls=%async_computation.1 | async-start | bytes 2883584 | tf_op jit(solution)/shard_map/all_to_all | solution.py:139
  50.6 0.7 all-gather.2.cloned.1.call-update
  51.3 20.9 %all-to-all-done.1 = bf16[8,704,128]{2,1,0:T(8,128)(2,1)S(1)} async-done(((bf16[8,704,128]{2,1,0:T(8,128)(2,1)}), bf16[8,704,128]{2,1,0:T(8,128)(2,1)S(1)}, u32[]{:S(2)}, u32[]{:S(2)}) %all-to-all-start.1) | async-done | bytes 1441824 | tf_op jit(solution)/shard_map/all_to_all | solution.py:139
  72.3 1.9 %collective-permute-start.3 = (bf16[8,704,128]{2,1,0:T(8,128)(2,1)S(1)}, bf16[8,704,128]{2,1,0:T(8,128)(2,1)}, u32[]{:S(2)}, u32[]{:S(2)}) collective-permute-start(bf16[8,704,128]{2,1,0:T(8,128)(2,1)S(1)} %all-to-all-done.1), channel_id=1, source_target_pairs={{0,8},{8,0},{1,9},{9,1},{2,10},{10,2},{3,11},{11,3},{4,12},{12,4},... | collective-permute-start | bytes 4325384 | tf_op jit(solution)/shard_map/ppermute | solution.py:147
  74.8 0.6 fusion.32
  75.4 5.1 %all-to-all-start.2 = ((bf16[32,80,128]{2,1,0:T(8,128)(2,1)}), bf16[32,80,128]{2,1,0:T(8,128)(2,1)S(1)}, u32[]{:S(2)}, u32[]{:S(2)}) async-start(bf16[32,80,128]{2,1,0:T(8,128)(2,1)} %fusion.4), calls=%async_computation.2 | async-start | bytes 1310720 | tf_op jit(solution)/shard_map/all_to_all | solution.py:145
  80.5 2.3 %maximum_select_fusion = bf16[2,8,704,128]{3,2,1,0:T(8,128)(2,1)S(1)} fusion(bf16[1,8,704,128]{3,2,1,0:T(8,128)(2,1)} %bitcast.13, bf16[1,8,704,128]{3,2,1,0:T(8,128)(2,1)S(1)} %bitcast.140, pred[]{:T(512)S(6)} %eq.29), kind=kLoop, calls=%fused_computation.8 | loop fusion | flops 4325376 | bytes 5767169 | tf_op jit(solution)/shard_map/jit(_where)/select_n | solution.py:40
  83.7 1.9 %multiply_reduce_fusion.2 = (f32[4,24]{1,0:T(4,128)S(1)}, f32[4,24]{1,0:T(4,128)S(1)}, f32[4,1,24,128]{3,2,1,0:T(8,128)S(1)}) fusion(f32[4,1,24,128]{3,2,1,0:T(8,128)S(1)} %bitcast.161, f32[128]{0:T(128)S(1)} %get-tuple-element.62, bf16[4,2,24,5120]{3,2,1,0:T(8,128)(2,1)} %bitcast.148, bf16[5120,128,1,1]{1,0,3,2:T(8,128)(2,1)S(1)} %bitcast.144), kind=kOutput, calls=%fused_computation.50 | convolution fusion | flops 125890368 | bytes 3376384 | tf_op jit(solution)/shard_map/slice | solution.py:158
  85.7 1.4 %multiply_reduce_fusion.3 = (f32[4,24]{1,0:T(4,128)S(1)}, f32[4,24]{1,0:T(4,128)S(1)}, f32[4,1,24,128]{3,2,1,0:T(8,128)S(1)}) fusion(f32[4,1,24,128]{3,2,1,0:T(8,128)} %bitcast.160, f32[128]{0:T(128)S(1)} %get-tuple-element.63, bf16[4,2,24,5120]{3,2,1,0:T(8,128)(2,1)S(1)} %bitcast.149, bf16[5120,128,1,1]{1,0,3,2:T(8,128)(2,1)S(1)} %bitcast.142), kind=kOutput, calls=%fused_computation.51 | convolution fusion | flops 125890368 | bytes 3376384 | tf_op jit(solution)/shard_map/slice | solution.py:158
  87.2 8.3 %psum.7 = f32[2,96]{1,0:T(2,128)S(1)} all-reduce(f32[2,96]{1,0:T(2,128)S(1)} %pad_maximum_fusion.3), channel_id=1, replica_groups=mesh['z'=8,'yl'=4,'c'=2,'x'=4,'yh'=2] {'x'}, use_global_device_ids=true, to_apply=%region_5.6 | all-reduce | flops 192 | bytes 1536 | tf_op jit(solution)/shard_map/psum | solution.py:166
  95.8 0.5 fusion.20
  96.4 0.6 fusion
  97.1 2.6 %collective-permute-start.5 = (bf16[24,5120]{1,0:T(8,128)(2,1)S(1)}, bf16[24,5120]{1,0:T(8,128)(2,1)S(1)}, u32[]{:S(2)}, u32[]{:S(2)}) collective-permute-start(bf16[24,5120]{1,0:T(8,128)(2,1)S(1)} %get-tuple-element.51), channel_id=1, source_target_pairs={{0,2},{2,4},{4,6},{6,0},{1,3},{3,5},{5,7},{7,1},{8,10},{10,12},{12... | collective-permute-start | bytes 737288 | tf_op jit(solution)/shard_map/ppermute | solution.py:84
  99.7 3.4 %collective-permute-start.6 = (bf16[24,5120]{1,0:T(8,128)(2,1)S(1)}, bf16[24,5120]{1,0:T(8,128)(2,1)S(1)}, u32[]{:S(2)}, u32[]{:S(2)}) collective-permute-start(bf16[24,5120]{1,0:T(8,128)(2,1)S(1)} %get-tuple-element.53), channel_id=1, source_target_pairs={{0,6},{2,0},{4,2},{6,4},{1,7},{3,1},{5,3},{7,5},{8,14},{10,8},{12,... | collective-permute-start | bytes 737288 | tf_op jit(solution)/shard_map/ppermute | solution.py:84
  103.1 5.8 %collective-permute-start.7 = (bf16[24,5120]{1,0:T(8,128)(2,1)S(1)}, bf16[24,5120]{1,0:T(8,128)(2,1)S(1)}, u32[]{:S(2)}, u32[]{:S(2)}) collective-permute-start(bf16[24,5120]{1,0:T(8,128)(2,1)S(1)} %get-tuple-element.52), channel_id=1, source_target_pairs={{0,4},{2,6},{4,0},{6,2},{1,5},{3,7},{5,1},{7,3},{8,12},{10,14},{12... | collective-permute-start | bytes 737288 | tf_op jit(solution)/shard_map/ppermute | solution.py:84
  109.0 5.2 %collective-permute-start.4 = (bf16[104,128]{1,0:T(8,128)(2,1)S(1)}, bf16[104,128]{1,0:T(8,128)(2,1)S(1)}, u32[]{:S(2)}, u32[]{:S(2)}) collective-permute-start(bf16[104,128]{1,0:T(8,128)(2,1)S(1)} %maximum_select_fusion.2), channel_id=1, source_target_pairs={{0,1},{1,0},{2,3},{3,2},{4,5},{5,4},{6,7},{7,6},{8,9},{9,8},{10,11... | collective-permute-start | bytes 79880 | tf_op jit(solution)/shard_map/ppermute | solution.py:185
  114.3 0.6 multiply_subtract_fusion.1
  115.0 0.8 fusion.7
  115.9 0.7 multiply_subtract_fusion
  116.6 2.1 %collective-permute-done.4 = bf16[104,128]{1,0:T(8,128)(2,1)S(1)} collective-permute-done((bf16[104,128]{1,0:T(8,128)(2,1)S(1)}, bf16[104,128]{1,0:T(8,128)(2,1)S(1)}, u32[]{:S(2)}, u32[]{:S(2)}) %collective-permute-start.4) | collective-permute-done | bytes 26656 | tf_op jit(solution)/shard_map/ppermute | solution.py:185
  119.2 2.0 %fusion.1 = bf16[1,5120,128]{2,1,0:T(8,128)(2,1)} fusion(bf16[192,5120]{1,0:T(8,128)(2,1)S(1)} %copy-done.4, bf16[192,128]{1,0:T(8,128)(2,1)S(1)} %bitcast.155), kind=kOutput, calls=%fused_computation.3 | convolution fusion | flops 252313600 | bytes 3325952 | tf_op jit(solution)/shard_map/dot_general | solution.py:192
  (68 shorter events, 2.8 us)
Async XLA Ops:
  7.2 25.0 %copy-start.6 = (bf16[24,5120]{1,0:T(8,128)(2,1)S(1)}, bf16[24,5120]{1,0:T(8,128)(2,1)}, u32[]{:S(2)}) copy-start(bf16[24,5120]{1,0:T(8,128)(2,1)} %param.10) | copy-start | bytes 737284
  7.2 13.9 %copy-start.1 = (f32[2,1]{0,1:T(1,128)S(1)}, f32[2,1]{0,1:T(1,128)}, u32[]{:S(2)}) copy-start(f32[2,1]{0,1:T(1,128)} %param.15) | copy-start | bytes 28
  7.2 13.9 %copy-start.2 = (f32[1,128,1]{1,2,0:T(1,128)S(1)}, f32[1,128,1]{1,2,0:T(1,128)}, u32[]{:S(2)}) copy-start(f32[1,128,1]{1,2,0:T(1,128)} %param.19) | copy-start | bytes 1540
  7.2 13.9 %copy-start = (f32[80,128]{1,0:T(8,128)S(1)}, f32[80,128]{1,0:T(8,128)}, u32[]{:S(2)}) copy-start(f32[80,128]{1,0:T(8,128)} %weight_ref.1) | copy-start | bytes 122884
  7.2 25.0 %collective-permute-start = (bf16[24,5120]{1,0:T(8,128)(2,1)}, bf16[24,5120]{1,0:T(8,128)(2,1)}, u32[]{:S(2)}, u32[]{:S(2)}) collective-permute-start(bf16[24,5120]{1,0:T(8,128)(2,1)} %param.10), channel_id=1, source_target_pairs={{0,1},{1,0},{2,3},{3,2},{4,5},{5,4},{6,7},{7,6},{8,9},{9,8},{10,11... | collective-permute-start | bytes 737288 | tf_op jit(solution)/shard_map/ppermute | solution.py:108
  15.0 17.2 %collective-permute-start.2 = (bf16[4,24,128]{2,1,0:T(8,128)(2,1)S(1)}, bf16[4,24,128]{2,1,0:T(8,128)(2,1)S(1)}, u32[]{:S(2)}, u32[]{:S(2)}) collective-permute-start(bf16[4,24,128]{2,1,0:T(8,128)(2,1)S(1)} %get-tuple-element.61), channel_id=1, source_target_pairs={{0,1},{1,0},{2,3},{3,2},{4,5},{5,4},{6,7},{7,6},{8,9},{9,8},{10,11... | collective-permute-start | bytes 73736 | tf_op jit(solution)/shard_map/ppermute | solution.py:134
  17.9 16.1 %copy-start.5 = (bf16[1,5120,128]{2,1,0:T(8,128)(2,1)S(1)}, bf16[1,5120,128]{2,1,0:T(8,128)(2,1)}, u32[]{:S(2)}) copy-start(bf16[1,5120,128]{2,1,0:T(8,128)(2,1)} %param.18) | copy-start | bytes 3932164
  19.1 14.9 %collective-permute-start.1 = (bf16[32,80,128]{2,1,0:T(8,128)(2,1)S(1)}, bf16[32,80,128]{2,1,0:T(8,128)(2,1)S(1)}, u32[]{:S(2)}, u32[]{:S(2)}) collective-permute-start(bf16[32,80,128]{2,1,0:T(8,128)(2,1)S(1)} %dynamic-slice_bitcast_fusion), channel_id=1, source_target_pairs={{0,8},{8,0},{1,9},{9,1},{2,10},{10,2},{3,11},{11,3},{4,12},{12,4},... | collective-permute-start | bytes 1966088 | tf_op jit(solution)/shard_map/ppermute | solution.py:130
  21.9 19.9 %all-to-all-start = ((bf16[8,88,128]{2,1,0:T(8,128)(2,1)}), bf16[8,88,128]{2,1,0:T(8,128)(2,1)S(1)}, u32[]{:S(2)}, u32[]{:S(2)}) async-start(bf16[8,88,128]{2,1,0:T(8,128)(2,1)} %shard_map.169), calls=%async_computation | async-start | bytes 360448 | tf_op jit(solution)/shard_map/all_to_all | solution.py:124
  43.1 29.2 %all-to-all-start.1 = ((bf16[8,704,128]{2,1,0:T(8,128)(2,1)}), bf16[8,704,128]{2,1,0:T(8,128)(2,1)S(1)}, u32[]{:S(2)}, u32[]{:S(2)}) async-start(bf16[8,704,128]{2,1,0:T(8,128)(2,1)} %broadcast_in_dim.57), calls=%async_computation.1 | async-start | bytes 2883584 | tf_op jit(solution)/shard_map/all_to_all | solution.py:139
  50.6 33.1 %all-gather.2.cloned.1.call-start = ((), (), s32[]{:S(2)}) async-start(), calls=%async_computation.3 | async-start | bytes 2457600 | tf_op jit(solution)/shard_map/all_gather | solution.py:138
  72.3 8.2 %collective-permute-start.3 = (bf16[8,704,128]{2,1,0:T(8,128)(2,1)S(1)}, bf16[8,704,128]{2,1,0:T(8,128)(2,1)}, u32[]{:S(2)}, u32[]{:S(2)}) collective-permute-start(bf16[8,704,128]{2,1,0:T(8,128)(2,1)S(1)} %all-to-all-done.1), channel_id=1, source_target_pairs={{0,8},{8,0},{1,9},{9,1},{2,10},{10,2},{3,11},{11,3},{4,12},{12,4},... | collective-permute-start | bytes 4325384 | tf_op jit(solution)/shard_map/ppermute | solution.py:147
  75.4 40.4 %all-to-all-start.2 = ((bf16[32,80,128]{2,1,0:T(8,128)(2,1)}), bf16[32,80,128]{2,1,0:T(8,128)(2,1)S(1)}, u32[]{:S(2)}, u32[]{:S(2)}) async-start(bf16[32,80,128]{2,1,0:T(8,128)(2,1)} %fusion.4), calls=%async_computation.2 | async-start | bytes 1310720 | tf_op jit(solution)/shard_map/all_to_all | solution.py:145
  83.7 1.9 %copy-start.3 = (bf16[192,5120]{1,0:T(8,128)(2,1)S(1)}, bf16[192,5120]{1,0:T(8,128)(2,1)}, u32[]{:S(2)}) copy-start(bf16[192,5120]{1,0:T(8,128)(2,1)} %all-gather.2.cloned.1.call-done) | copy-start | bytes 5898244
  96.9 12.0 %copy-start.9 = (pred[8]{0:T(512)(128)(4,1)S(1)}, pred[8]{0:T(512)(128)(4,1)}, u32[]{:S(2)}) copy-start(pred[8]{0:T(512)(128)(4,1)} %get-tuple-element.77) | copy-start | bytes 28
  97.0 12.0 %copy-start.10 = (pred[8]{0:T(512)(128)(4,1)S(1)}, pred[8]{0:T(512)(128)(4,1)}, u32[]{:S(2)}) copy-start(pred[8]{0:T(512)(128)(4,1)} %get-tuple-element.78) | copy-start | bytes 28
  97.0 17.3 %copy-start.11 = (f32[2,1]{0,1:T(1,128)S(1)}, f32[2,1]{0,1:T(1,128)}, u32[]{:S(2)}) copy-start(f32[2,1]{0,1:T(1,128)} %param.16) | copy-start | bytes 28
  97.0 17.3 %copy-start.12 = (f32[2,1]{0,1:T(1,128)S(1)}, f32[2,1]{0,1:T(1,128)}, u32[]{:S(2)}) copy-start(f32[2,1]{0,1:T(1,128)} %param.17) | copy-start | bytes 28
  97.0 18.9 %copy-start.7 = (f32[80,128]{1,0:T(8,128)S(1)}, f32[80,128]{1,0:T(8,128)}, u32[]{:S(2)}) copy-start(f32[80,128]{1,0:T(8,128)} %param.13) | copy-start | bytes 122884
  97.0 18.9 %copy-start.8 = (f32[80,128]{1,0:T(8,128)S(1)}, f32[80,128]{1,0:T(8,128)}, u32[]{:S(2)}) copy-start(f32[80,128]{1,0:T(8,128)} %param.14) | copy-start | bytes 122884
  97.1 22.1 %copy-start.4 = (bf16[192,5120]{1,0:T(8,128)(2,1)S(1)}, bf16[192,5120]{1,0:T(8,128)(2,1)}, u32[]{:S(2)}) copy-start(bf16[192,5120]{1,0:T(8,128)(2,1)} %all-gather.2.cloned.1.call-done) | copy-start | bytes 5898244
  97.1 17.9 %collective-permute-start.5 = (bf16[24,5120]{1,0:T(8,128)(2,1)S(1)}, bf16[24,5120]{1,0:T(8,128)(2,1)S(1)}, u32[]{:S(2)}, u32[]{:S(2)}) collective-permute-start(bf16[24,5120]{1,0:T(8,128)(2,1)S(1)} %get-tuple-element.51), channel_id=1, source_target_pairs={{0,2},{2,4},{4,6},{6,0},{1,3},{3,5},{5,7},{7,1},{8,10},{10,12},{12... | collective-permute-start | bytes 737288 | tf_op jit(solution)/shard_map/ppermute | solution.py:84
  99.7 15.3 %collective-permute-start.6 = (bf16[24,5120]{1,0:T(8,128)(2,1)S(1)}, bf16[24,5120]{1,0:T(8,128)(2,1)S(1)}, u32[]{:S(2)}, u32[]{:S(2)}) collective-permute-start(bf16[24,5120]{1,0:T(8,128)(2,1)S(1)} %get-tuple-element.53), channel_id=1, source_target_pairs={{0,6},{2,0},{4,2},{6,4},{1,7},{3,1},{5,3},{7,5},{8,14},{10,8},{12,... | collective-permute-start | bytes 737288 | tf_op jit(solution)/shard_map/ppermute | solution.py:84
  103.1 11.9 %collective-permute-start.7 = (bf16[24,5120]{1,0:T(8,128)(2,1)S(1)}, bf16[24,5120]{1,0:T(8,128)(2,1)S(1)}, u32[]{:S(2)}, u32[]{:S(2)}) collective-permute-start(bf16[24,5120]{1,0:T(8,128)(2,1)S(1)} %get-tuple-element.52), channel_id=1, source_target_pairs={{0,4},{2,6},{4,0},{6,2},{1,5},{3,7},{5,1},{7,3},{8,12},{10,14},{12... | collective-permute-start | bytes 737288 | tf_op jit(solution)/shard_map/ppermute | solution.py:84
  109.0 9.7 %collective-permute-start.4 = (bf16[104,128]{1,0:T(8,128)(2,1)S(1)}, bf16[104,128]{1,0:T(8,128)(2,1)S(1)}, u32[]{:S(2)}, u32[]{:S(2)}) collective-permute-start(bf16[104,128]{1,0:T(8,128)(2,1)S(1)} %maximum_select_fusion.2), channel_id=1, source_target_pairs={{0,1},{1,0},{2,3},{3,2},{4,5},{5,4},{6,7},{7,6},{8,9},{9,8},{10,11... | collective-permute-start | bytes 79880 | tf_op jit(solution)/shard_map/ppermute | solution.py:185
Sparse Core Ops, SparseCore 0:
  53.6 29.5 all-gather.1
